TPU v7x, 32 devices: a whole 2x2x4 slice. The times are simulated.
32 devices in a mesh: dp: 8 (over y, x, core), tensor: 4 (over z).
Axes of the slice: x: 2, y: 2, z: 4, core: 2. Of those that a mesh axis runs over, the one named last changes fastest.
Arguments:
- activations: bfloat16 [584, 16, 1024], P('tensor', 'dp'), may hold values from -6 to 6
- cotangent: bfloat16 [584, 16, 1024], P('tensor', 'dp'), may hold values from -6 to 6
- token_valid: int32 [16, 584], P('dp'), may hold values from 0 to 1, as said below
- image_counts: int32 [8], P('dp'), may hold values from 1 to 2, as said below
- pre_gain: bfloat16 [1024], P('dp'), may hold values from 0.5 to 1.5
- pre_shift: bfloat16 [1024], P('dp'), may hold values from -3 to 3
- attn_weight: bfloat16 [3, 1024, 1024], P(None, 'dp', 'tensor'), may hold values from -0.1875 to 0.1875
- attn_bias: bfloat16 [2, 1024], P(None, 'tensor'), may hold values from -3 to 3
- proj_weight: bfloat16 [1024, 1024], P('tensor', 'dp'), may hold values from -0.5 to 0.5
- proj_bias: bfloat16 [1024], P('dp'), may hold values from -3 to 3
- mid_gain: bfloat16 [1024], P('dp'), may hold values from 0.5 to 1.5
- mid_shift: bfloat16 [1024], P('dp'), may hold values from -3 to 3
- up_weight: bfloat16 [1024, 4096], P('dp', 'tensor'), may hold values from -0.1875 to 0.1875
- up_bias: bfloat16 [4096], P('tensor'), may hold values from -3 to 3
- down_weight: bfloat16 [4096, 1024], P('tensor', 'dp'), may hold values from -0.09375 to 0.09375
- down_bias: bfloat16 [1024], P('dp'), may hold values from -3 to 3
Outputs:
- block_out: bfloat16 [584, 16, 1024], P('tensor', 'dp')
- input_grad: float32 [584, 16, 1024], P('tensor', 'dp')
- pregain_grad: float32 [1024], P('dp')
- preshift_grad: float32 [1024], P('dp')
- attnweight_grad: float32 [3, 1024, 1024], P(None, 'dp', 'tensor')
- attnbias_grad: float32 [2, 1024], P(None, 'tensor')
- projweight_grad: float32 [1024, 1024], P('tensor', 'dp')
- projbias_grad: float32 [1024], P('dp')
- midgain_grad: float32 [1024], P('dp')
- midshift_grad: float32 [1024], P('dp')
- upweight_grad: float32 [1024, 4096], P('dp', 'tensor')
- upbias_grad: float32 [4096], P('tensor')
- downweight_grad: float32 [4096, 1024], P('tensor', 'dp')
- downbias_grad: float32 [1024], P('dp')
Inputs may be any that keep to these rules, and one draw needn't show every extreme that they name: `token_valid`: the valid tokens of each image are a leading run of 292 or more positions, followed only by padding. The slots of a dp index that hold images are its first image_counts ones; in every draw some dp index holds 2 images.
All inputs are finite; a program needn't handle non-finite values.
Results may differ from a plain program's by a relative error of at most 0.012.
Values may be sent and summed in bfloat16 or wider, within the bound.
A program may use at most 192 MiB of HBM per device.

v0:
```python
import jax
import jax.numpy as jnp
from jax import lax
from jax.sharding import PartitionSpec as P

D = 1024
H = 16
HD = 64
MB = 2


EPS = 1e-06
NEG = -1000000000.0


def layer_norm(values, gain, shift):
    center = values - jnp.mean(values, axis=-1, keepdims=True)
    spread = jnp.mean(center * center, axis=-1, keepdims=True)
    return center * lax.rsqrt(spread + EPS) * gain + shift


def gelu_exact(values):
    return jax.nn.gelu(values, approximate=False)


def per_device(
    activations,
    cotangent,
    token_valid,
    image_counts,
    pre_gain,
    pre_shift,
    attn_weight,
    attn_bias,
    proj_weight,
    proj_bias,
    mid_gain,
    mid_shift,
    up_weight,
    up_bias,
    down_weight,
    down_bias,
):
    f32 = jnp.float32
    bf16 = jnp.bfloat16
    tensor_size = lax.axis_size("tensor")
    local_rows = activations.shape[0]
    slots = activations.shape[1]
    per_micro = slots // MB
    heads_here = H // tensor_size
    width_here = attn_weight.shape[2]
    hidden_here = up_weight.shape[1]
    scale = HD ** (-0.5)
    first_row = lax.axis_index("tensor") * local_rows
    my_valid = lax.dynamic_slice_in_dim(token_valid, first_row, local_rows, 1).astype(f32)
    slot_live = (jnp.arange(slots, dtype=jnp.int32) < image_counts[0]).astype(f32)
    attn_bias_f = attn_bias.astype(f32)
    up_bias_f = up_bias.astype(f32)
    acc_attn = jnp.zeros((3, D, width_here), f32)
    acc_proj = jnp.zeros((width_here, D), f32)
    acc_up = jnp.zeros((D, hidden_here), f32)
    acc_down = jnp.zeros((hidden_here, D), f32)
    acc_attn_bias = jnp.zeros((2, width_here), f32)
    acc_up_bias = jnp.zeros((hidden_here,), f32)
    acc_vectors = [jnp.zeros((D,), f32) for unused in range(6)]
    block_parts = []
    input_parts = []
    for micro_step in range(MB):
        gathered = (
            lax.all_gather(attn_weight, "dp", axis=1, tiled=True),
            lax.all_gather(proj_weight, "dp", axis=1, tiled=True),
            lax.all_gather(up_weight, "dp", axis=0, tiled=True),
            lax.all_gather(down_weight, "dp", axis=1, tiled=True),
            lax.all_gather(pre_gain, "dp", axis=0, tiled=True),
            lax.all_gather(pre_shift, "dp", axis=0, tiled=True),
            lax.all_gather(proj_bias, "dp", axis=0, tiled=True),
            lax.all_gather(mid_gain, "dp", axis=0, tiled=True),
            lax.all_gather(mid_shift, "dp", axis=0, tiled=True),
            lax.all_gather(down_bias, "dp", axis=0, tiled=True),
        )
        qkv_full, proj_full, upw_full, downw_full = (
            gathered[0],
            gathered[1],
            gathered[2],
            gathered[3],
        )
        gain_one, shift_one, proj_bias_f, gain_two, shift_two, down_bias_f = [
            item.astype(f32) for item in gathered[4:]
        ]
        offset = micro_step * per_micro
        inputs_f = activations[:, offset : offset + per_micro].astype(f32)
        key_valid = token_valid[offset : offset + per_micro]
        key_bias = jnp.where(key_valid > 0, 0.0, NEG).astype(f32)
        out_mask = jnp.transpose(
            slot_live[offset : offset + per_micro][:, None] * my_valid[offset : offset + per_micro]
        )[:, :, None]
        normed = layer_norm(inputs_f, gain_one, shift_one).astype(bf16)
        normed_all = lax.all_gather(normed, "tensor", axis=0, tiled=True)
        full_rows = normed_all.shape[0]
        projected = jnp.einsum("sid,cde->csie", normed_all, qkv_full, preferred_element_type=f32)
        queries = (
            (projected[0] + attn_bias_f[0])
            .astype(bf16)
            .reshape(full_rows, per_micro, heads_here, HD)
        )
        keys = projected[1].astype(bf16).reshape(full_rows, per_micro, heads_here, HD)
        values = (
            (projected[2] + attn_bias_f[1])
            .astype(bf16)
            .reshape(full_rows, per_micro, heads_here, HD)
        )

        def scores_of(query_part, key_part):
            raw = jnp.einsum("qihe,kihe->ihqk", query_part, key_part, preferred_element_type=f32)
            return raw * scale + key_bias[:, None, None, :]

        scores = scores_of(queries, keys)
        top = jnp.max(scores, axis=-1, keepdims=True)
        expo = jnp.exp(scores - top)
        total = jnp.sum(expo, axis=-1, keepdims=True)
        logsum = top + jnp.log(total)
        probs_low = (expo / total).astype(bf16)
        attended = (
            jnp.einsum("ihqk,kihe->qihe", probs_low, values, preferred_element_type=f32)
            .astype(bf16)
            .reshape(full_rows, per_micro, width_here)
        )
        resid = (
            inputs_f
            + lax.psum_scatter(
                jnp.einsum("sie,ed->sid", attended, proj_full, preferred_element_type=f32),
                "tensor",
                scatter_dimension=0,
                tiled=True,
            )
            + proj_bias_f
        )
        normed2 = layer_norm(resid, gain_two, shift_two).astype(bf16)
        normed2_all = lax.all_gather(normed2, "tensor", axis=0, tiled=True)
        hidden_pre = (
            jnp.einsum("sid,df->sif", normed2_all, upw_full, preferred_element_type=f32) + up_bias_f
        )
        hidden = gelu_exact(hidden_pre).astype(bf16)
        mlp_out = (
            lax.psum_scatter(
                jnp.einsum("sif,fd->sid", hidden, downw_full, preferred_element_type=f32).astype(
                    jnp.bfloat16
                ),
                "tensor",
                scatter_dimension=0,
                tiled=True,
            ).astype(jnp.float32)
            + down_bias_f
        )
        block_parts.append(((resid + mlp_out) * out_mask).astype(bf16))
        outer = cotangent[:, offset : offset + per_micro].astype(f32) * out_mask
        mlp_grad = outer.astype(bf16)
        acc_vectors[5] = acc_vectors[5] + jnp.sum(mlp_grad.astype(f32), axis=(0, 1))
        mlp_grad_all = lax.all_gather(mlp_grad, "tensor", axis=0, tiled=True)
        acc_down = acc_down + jnp.einsum(
            "sif,sid->fd", hidden, mlp_grad_all, preferred_element_type=f32
        )
        hidden_grad = jnp.einsum(
            "sid,fd->sif", mlp_grad_all, downw_full, preferred_element_type=f32
        )
        unused, gelu_back = jax.vjp(gelu_exact, hidden_pre)
        pre_grad = gelu_back(hidden_grad)[0].astype(bf16)
        acc_up_bias = acc_up_bias + jnp.sum(pre_grad.astype(f32), axis=(0, 1))
        acc_up = acc_up + jnp.einsum(
            "sid,sif->df", normed2_all, pre_grad, preferred_element_type=f32
        )
        normed2_grad = lax.psum_scatter(
            jnp.einsum("sif,df->sid", pre_grad, upw_full, preferred_element_type=f32),
            "tensor",
            scatter_dimension=0,
            tiled=True,
        )
        unused, second_back = jax.vjp(layer_norm, resid, gain_two, shift_two)
        resid_part, gain_two_grad, shift_two_grad = second_back(normed2_grad)
        acc_vectors[3] = acc_vectors[3] + gain_two_grad
        acc_vectors[4] = acc_vectors[4] + shift_two_grad
        resid_grad = outer + resid_part
        branch_grad = resid_grad.astype(bf16)
        acc_vectors[2] = acc_vectors[2] + jnp.sum(branch_grad.astype(f32), axis=(0, 1))
        branch_all = lax.all_gather(branch_grad, "tensor", axis=0, tiled=True)
        acc_proj = acc_proj + jnp.einsum(
            "sie,sid->ed", attended, branch_all, preferred_element_type=f32
        )
        att_grad = (
            jnp.einsum("sid,ed->sie", branch_all, proj_full, preferred_element_type=f32)
            .astype(bf16)
            .reshape(full_rows, per_micro, heads_here, HD)
        )
        probs = jnp.exp(scores_of(queries, keys) - logsum)
        probs_again = probs.astype(bf16)
        value_grad = jnp.einsum(
            "ihqk,qihe->kihe", probs_again, att_grad, preferred_element_type=f32
        ).astype(bf16)
        prob_grad = jnp.einsum("qihe,kihe->ihqk", att_grad, values, preferred_element_type=f32)
        score_grad = (
            probs * (prob_grad - jnp.sum(prob_grad * probs, axis=-1, keepdims=True))
        ).astype(bf16)
        query_grad = (
            jnp.einsum("ihqk,kihe->qihe", score_grad, keys, preferred_element_type=f32) * scale
        ).astype(bf16)
        key_grad = (
            jnp.einsum("ihqk,qihe->kihe", score_grad, queries, preferred_element_type=f32) * scale
        ).astype(bf16)
        qkv_grad = jnp.stack([query_grad, key_grad, value_grad]).reshape(
            3, full_rows, per_micro, width_here
        )
        acc_attn_bias = acc_attn_bias + jnp.stack(
            [
                jnp.sum(qkv_grad[0].astype(f32), axis=(0, 1)),
                jnp.sum(qkv_grad[2].astype(f32), axis=(0, 1)),
            ]
        )
        acc_attn = acc_attn + jnp.einsum(
            "sid,csie->cde", normed_all, qkv_grad, preferred_element_type=f32
        )
        normed_grad = lax.psum_scatter(
            jnp.einsum("csie,cde->sid", qkv_grad, qkv_full, preferred_element_type=f32),
            "tensor",
            scatter_dimension=0,
            tiled=True,
        )
        unused, first_back = jax.vjp(layer_norm, inputs_f, gain_one, shift_one)
        input_part, gain_one_grad, shift_one_grad = first_back(normed_grad)
        acc_vectors[0] = acc_vectors[0] + gain_one_grad
        acc_vectors[1] = acc_vectors[1] + shift_one_grad
        input_parts.append(resid_grad + input_part)
    summed = lax.psum(
        (
            acc_vectors[0],
            acc_vectors[1],
            acc_vectors[2],
            acc_vectors[3],
            acc_vectors[4],
            acc_vectors[5],
        ),
        "tensor",
    )
    owned = (
        lax.psum_scatter(acc_attn, "dp", scatter_dimension=1, tiled=True),
        lax.psum_scatter(acc_proj, "dp", scatter_dimension=1, tiled=True),
        lax.psum_scatter(acc_up, "dp", scatter_dimension=0, tiled=True),
        lax.psum_scatter(acc_down, "dp", scatter_dimension=1, tiled=True),
        lax.psum_scatter(summed[0], "dp", scatter_dimension=0, tiled=True),
        lax.psum_scatter(summed[1], "dp", scatter_dimension=0, tiled=True),
        lax.psum_scatter(summed[2], "dp", scatter_dimension=0, tiled=True),
        lax.psum_scatter(summed[3], "dp", scatter_dimension=0, tiled=True),
        lax.psum_scatter(summed[4], "dp", scatter_dimension=0, tiled=True),
        lax.psum_scatter(summed[5], "dp", scatter_dimension=0, tiled=True),
    )
    bias_sums = lax.psum((acc_attn_bias, acc_up_bias), "dp")
    block_out = jnp.concatenate(block_parts, axis=1)
    input_grad = jnp.concatenate(input_parts, axis=1)
    return (
        block_out,
        input_grad,
        owned[4],
        owned[5],
        owned[0],
        bias_sums[0],
        owned[1],
        owned[6],
        owned[7],
        owned[8],
        owned[2],
        bias_sums[1],
        owned[3],
        owned[9],
    )


def solution(mesh):
    return jax.shard_map(
        per_device,
        mesh=mesh,
        in_specs=(
            P("tensor", "dp", None),
            P("tensor", "dp", None),
            P("dp", None),
            P("dp"),
            P("dp"),
            P("dp"),
            P(None, "dp", "tensor"),
            P(None, "tensor"),
            P("tensor", "dp"),
            P("dp"),
            P("dp"),
            P("dp"),
            P("dp", "tensor"),
            P("tensor"),
            P("tensor", "dp"),
            P("dp"),
        ),
        out_specs=(
            P("tensor", "dp", None),
            P("tensor", "dp", None),
            P("dp"),
            P("dp"),
            P(None, "dp", "tensor"),
            P(None, "tensor"),
            P("tensor", "dp"),
            P("dp"),
            P("dp"),
            P("dp"),
            P("dp", "tensor"),
            P("tensor"),
            P("tensor", "dp"),
            P("dp"),
        ),
        check_vma=False,
    )
```

profile of v0, /device:TPU:0, one launch (start us, length us, event | category | flops | bytes accessed | tf_op | source)
XLA Modules:
  0.0 1428.0 jit_solution(13615151279646853309)
XLA Ops:
  10.4 10.3 all-gather
  20.7 8.6 all-gather.1
  39.6 9.6 all_gather.68
  49.2 40.0 %all-gather.28.cloned.1.call-done = bf16[584,1,1024]{2,1,0:T(2,128)(2,1)} async-done(((bf16[146,1,1024]{2,1,0:T(2,128)(2,1)}), bf16[584,1,1024]{2,1,0:T(2,128)(2,1)}) %all-gather.28.cloned.1.call-update) | async-done | bytes 1196048 | tf_op jit(solution)/shard_map/all_gather | solution.py:98
  89.3 26.4 %all-gather.20.cloned.1.call-done = bf16[3,1024,256]{2,1,0:T(8,128)(2,1)} async-done(((bf16[3,128,256]{2,1,0:T(8,128)(2,1)}), bf16[3,1024,256]{2,1,0:T(8,128)(2,1)}) %all-gather.20.cloned.1.call-update) | async-done | bytes 1572880 | tf_op jit(solution)/shard_map/all_gather | solution.py:70
  119.1 49.8 %all-gather.18.cloned.1.call-done = bf16[584,1,1024]{2,1,0:T(2,128)(2,1)} async-done(((bf16[146,1,1024]{2,1,0:T(2,128)(2,1)}), bf16[584,1,1024]{2,1,0:T(2,128)(2,1)}) %all-gather.18.cloned.1.call-update) | async-done | bytes 1196048 | tf_op jit(solution)/shard_map/all_gather | solution.py:98
  199.5 8.7 all-gather.2
  208.3 8.7 all-gather.3
  216.9 7.8 all-gather.4
  226.0 146.3 %all-reduce.30.cloned.1.call-done = (f32[584,1,1024]{2,1,0:T(1,128)}, f32[584,1,1024]{2,1,0:T(1,128)}) async-done(((f32[584,1,1024]{2,1,0:T(1,128)}, f32[584,1,1024]{2,1,0:T(1,128)}), (f32[584,1,1024]{2,1,0:T(1,128)}, f32[584,1,1024]{2,1,0:T(1,128)})) %all-reduce.30.cloned.1.call-update) | async-done | bytes 4784144
  385.8 15.3 %all-gather.24.cloned.1.call-done = bf16[1024,1024]{1,0:T(8,128)(2,1)} async-done(((bf16[128,1024]{1,0:T(8,128)(2,1)}), bf16[1024,1024]{1,0:T(8,128)(2,1)}) %all-gather.24.cloned.1.call-update) | async-done | bytes 2097168 | tf_op jit(solution)/shard_map/all_gather | solution.py:72
  401.1 52.6 %all-gather.30.cloned.1.call-done = bf16[584,1,1024]{2,1,0:T(2,128)(2,1)} async-done(((bf16[146,1,1024]{2,1,0:T(2,128)(2,1)}), bf16[584,1,1024]{2,1,0:T(2,128)(2,1)}) %all-gather.30.cloned.1.call-update) | async-done | bytes 1196048 | tf_op jit(solution)/shard_map/all_gather | solution.py:139
  458.8 47.0 %all-gather.22.cloned.1.call-done = bf16[584,1,1024]{2,1,0:T(2,128)(2,1)} async-done(((bf16[146,1,1024]{2,1,0:T(2,128)(2,1)}), bf16[584,1,1024]{2,1,0:T(2,128)(2,1)}) %all-gather.22.cloned.1.call-update) | async-done | bytes 1196048 | tf_op jit(solution)/shard_map/all_gather | solution.py:139
  505.7 16.0 %multiply_convert_fusion.3 = (bf16[584,1024]{1,0:T(8,128)(2,1)}, f32[584,1024]{1,0:T(8,128)}, bf16[584,1024]{1,0:T(8,128)(2,1)}, f32[584,1024]{1,0:T(8,128)}, f32[584,1024]{1,0:T(8,128)}) fusion(f32[1024]{0:T(1024)S(1)} %convert_element_type.338, f32[584,1024]{1,0:T(8,128)} %fusion.57, bf16[1024,1024]{1,0:T(8,128)(2,1)} %all-gather.24.cloned.1.call-done, ...), kind=kOutput, calls=%fused_computation.44 | convolution fusion | flops 1303674880 | bytes 15257600 | tf_op jit(solution)/shard_map/sid,df->sif/dot_general | solution.py:141
  521.8 13.0 all-gather.26.cloned.1.call-done
  541.9 48.2 %fusion.106 = (bf16[152,1024]{1,0:T(8,128)(2,1)S(1)}, bf16[152,1024]{1,0:T(8,128)(2,1)}) fusion(bf16[584,1,1024]{2,0,1:T(8,128)(2,1)} %fusion.27, bf16[584,1,1024]{2,0,1:T(8,128)(2,1)} %fusion.26), kind=kCustom, calls=%all-reduce-scatter.2 | all-reduce-scatter fusion | flops 1245185 | bytes 3015168
  595.6 8.7 all-gather.5
  615.9 8.2 multiply_convert_fusion.5
  628.0 47.2 %all-gather.32.cloned.1.call-done = bf16[584,1,1024]{2,1,0:T(2,128)(2,1)} async-done(((bf16[146,1,1024]{2,1,0:T(2,128)(2,1)}), bf16[584,1,1024]{2,1,0:T(2,128)(2,1)}) %all-gather.32.cloned.1.call-update) | async-done | bytes 1196048 | tf_op jit(solution)/shard_map/all_gather | solution.py:159
  675.2 6.1 convert_reduce_fusion.1
  687.6 38.9 %all-gather.36.cloned.1.call-done = bf16[584,1,1024]{2,1,0:T(2,128)(2,1)} async-done(((bf16[146,1,1024]{2,1,0:T(2,128)(2,1)}), bf16[584,1,1024]{2,1,0:T(2,128)(2,1)}) %all-gather.36.cloned.1.call-update) | async-done | bytes 1196048 | tf_op jit(solution)/shard_map/all_gather | solution.py:159
  726.5 6.1 convert_reduce_fusion
  739.2 173.2 %all-reduce.28.cloned.1.call-done = (f32[584,1,1024]{2,1,0:T(1,128)}, f32[584,1,1024]{2,1,0:T(1,128)}) async-done(((f32[584,1,1024]{2,1,0:T(1,128)}, f32[584,1,1024]{2,1,0:T(1,128)}), (f32[584,1,1024]{2,1,0:T(1,128)}, f32[584,1,1024]{2,1,0:T(1,128)})) %all-reduce.28.cloned.1.call-update) | async-done | bytes 4784144
  917.4 6.1 fusion.109
  929.7 46.1 %all-gather.34.cloned.1.call-done = bf16[584,1,1024]{2,1,0:T(2,128)(2,1)} async-done(((bf16[146,1,1024]{2,1,0:T(2,128)(2,1)}), bf16[584,1,1024]{2,1,0:T(2,128)(2,1)}) %all-gather.34.cloned.1.call-update) | async-done | bytes 1196048 | tf_op jit(solution)/shard_map/all_gather | solution.py:185
  990.3 37.4 %all-gather.38.cloned.1.call-done = bf16[584,1,1024]{2,1,0:T(2,128)(2,1)} async-done(((bf16[146,1,1024]{2,1,0:T(2,128)(2,1)}), bf16[584,1,1024]{2,1,0:T(2,128)(2,1)}) %all-gather.38.cloned.1.call-update) | async-done | bytes 1196048 | tf_op jit(solution)/shard_map/all_gather | solution.py:185
  1087.9 6.9 reduce-scatter.11.cloned.1.call-done
  1096.7 174.9 %all-reduce.26.cloned.1.call-done = (f32[584,1,1024]{2,1,0:T(1,128)}, f32[584,1,1024]{2,1,0:T(1,128)}) async-done(((f32[584,1,1024]{2,1,0:T(1,128)}, f32[584,1,1024]{2,1,0:T(1,128)}), (f32[584,1,1024]{2,1,0:T(1,128)}, f32[584,1,1024]{2,1,0:T(1,128)})) %all-reduce.26.cloned.1.call-update) | async-done | bytes 4784144
  1276.7 25.3 %all-reduce.16 = (f32[1024]{0:T(1024)S(1)}, f32[1024]{0:T(1024)S(1)}, f32[2,256]{1,0:T(2,128)}, f32[1024]{0:T(1024)S(1)}, f32[1024]{0:T(1024)S(1)}, /*index=5*/f...) all-reduce(f32[1024]{0:T(1024)S(1)} %add.380, ...), channel_id=10, replica_groups=mesh['dp'=8,'tensor'=4] {'dp'}, use_global_device_ids=true, to_apply=%region_33.34.clone | all-reduce | flops 7680 | bytes 61440
  1302.4 10.2 all-reduce.17
  1325.8 55.5 %reduce-scatter.15.cloned.1.call-done = f32[128,1024]{1,0:T(8,128)} async-done(((f32[1024,1024]{1,0:T(8,128)}), f32[128,1024]{1,0:T(8,128)}) %reduce-scatter.15.cloned.1.call-update) | async-done | bytes 524304 | tf_op jit(solution)/shard_map/reduce_scatter | solution.py:246
  1381.3 39.6 %reduce-scatter.13.cloned.1.call-done = f32[256,128]{1,0:T(8,128)} async-done(((f32[256,1024]{1,0:T(8,128)}), f32[256,128]{1,0:T(8,128)}) %reduce-scatter.13.cloned.1.call-update) | async-done | bytes 131088 | tf_op jit(solution)/shard_map/reduce_scatter | solution.py:245
  (322 shorter events, 211.1 us)
Async XLA Ops:
  7.2 82.1 %all-gather.28.cloned.1.call-start = ((), (), s32[]{:S(2)}) async-start(), calls=%async_computation.9 | async-start | bytes 2990080 | tf_op jit(solution)/shard_map/all_gather | solution.py:98
  34.5 84.5 %copy-start.48 = (f32[146]{0:T(256)}, f32[146]{0:T(256)S(1)}, u32[]{:S(2)}) copy-start(f32[146]{0:T(256)S(1)} %get-tuple-element.152) | copy-start | bytes 1756
  37.8 77.9 %all-gather.20.cloned.1.call-start = ((), (), s32[]{:S(2)}) async-start(), calls=%async_computation.5 | async-start | bytes 1769472 | tf_op jit(solution)/shard_map/all_gather | solution.py:70
  38.5 130.4 %all-gather.18.cloned.1.call-start = ((), (), s32[]{:S(2)}) async-start(), calls=%async_computation.4 | async-start | bytes 2990080 | tf_op jit(solution)/shard_map/all_gather | solution.py:98
  39.3 333.0 %all-reduce.30.cloned.1.call-start = ((), (), s32[]{:S(2)}) async-start(), calls=%async_computation.21 | async-start | bytes 9568256
  49.2 145.2 %copy-start.15 = (bf16[256,1024]{1,0:T(8,128)(2,1)}, bf16[256,1024]{1,0:T(8,128)(2,1)S(1)}, u32[]{:S(2)}) copy-start(bf16[256,1024]{1,0:T(8,128)(2,1)S(1)} %all_gather.68) | copy-start | bytes 1572868
  198.8 173.4 %copy-start.2 = (bf16[146,2,1024]{2,1,0:T(2,128)(2,1)S(1)}, bf16[146,2,1024]{2,1,0:T(2,128)(2,1)}, u32[]{:S(2)}) copy-start(bf16[146,2,1024]{2,1,0:T(2,128)(2,1)} %param.16) | copy-start | bytes 1794052
  198.9 202.2 %all-gather.24.cloned.1.call-start = ((), (), s32[]{:S(2)}) async-start(), calls=%async_computation.7 | async-start | bytes 2359296 | tf_op jit(solution)/shard_map/all_gather | solution.py:72
  199.5 254.2 %all-gather.30.cloned.1.call-start = ((), (), s32[]{:S(2)}) async-start(), calls=%async_computation.10 | async-start | bytes 2990080 | tf_op jit(solution)/shard_map/all_gather | solution.py:139
  382.7 123.1 %all-gather.22.cloned.1.call-start = ((), (), s32[]{:S(2)}) async-start(), calls=%async_computation.6 | async-start | bytes 2990080 | tf_op jit(solution)/shard_map/all_gather | solution.py:139
  383.4 151.4 %all-gather.26.cloned.1.call-start = ((), (), s32[]{:S(2)}) async-start(), calls=%async_computation.8 | async-start | bytes 2359296 | tf_op jit(solution)/shard_map/all_gather | solution.py:73
  384.2 291.0 %all-gather.32.cloned.1.call-start = ((), (), s32[]{:S(2)}) async-start(), calls=%async_computation.11 | async-start | bytes 2990080 | tf_op jit(solution)/shard_map/all_gather | solution.py:159
  541.9 53.6 %copy-start.56 = (bf16[128]{0:T(256)(128)(2,1)S(1)}, bf16[128]{0:T(256)(128)(2,1)}, u32[]{:S(2)}) copy-start(bf16[128]{0:T(256)(128)(2,1)} %param.31) | copy-start | bytes 772
  590.9 16.0 %collective-permute-start = (bf16[18,1024]{1,0:T(8,128)(2,1)S(1)}, bf16[18,1024]{1,0:T(8,128)(2,1)S(1)}, u32[]{:S(2)}, u32[]{:S(2)}) collective-permute-start(bf16[18,1024]{1,0:T(8,128)(2,1)S(1)} %slice.94), channel_id=1, source_target_pairs={{0,1},{1,2},{2,3},{4,5},{5,6},{6,7},{8,9},{9,10},{10,11},{12,13},{... | collective-permute-start | bytes 110600
  605.0 7.0 collective-permute-start.1
  624.1 57.2 %copy-start.9 = (f32[146,1,1024]{2,1,0:T(1,128)}, f32[146,1,1024]{2,1,0:T(1,128)S(1)}, u32[]{:S(2)}) copy-start(f32[146,1,1024]{2,1,0:T(1,128)S(1)} %get-tuple-element.173) | copy-start | bytes 1794052
  626.2 100.4 %all-gather.36.cloned.1.call-start = ((), (), s32[]{:S(2)}) async-start(), calls=%async_computation.13 | async-start | bytes 2990080 | tf_op jit(solution)/shard_map/all_gather | solution.py:159
  627.5 284.9 %all-reduce.28.cloned.1.call-start = ((), (), s32[]{:S(2)}) async-start(), calls=%async_computation.20 | async-start | bytes 9568256
  738.9 236.8 %all-gather.34.cloned.1.call-start = ((), (), s32[]{:S(2)}) async-start(), calls=%async_computation.12 | async-start | bytes 2990080 | tf_op jit(solution)/shard_map/all_gather | solution.py:185
  925.5 102.2 %all-gather.38.cloned.1.call-start = ((), (), s32[]{:S(2)}) async-start(), calls=%async_computation.14 | async-start | bytes 2990080 | tf_op jit(solution)/shard_map/all_gather | solution.py:185
  929.6 165.2 %reduce-scatter.11.cloned.1.call-start = ((), (), s32[]{:S(2)}) async-start(), calls=%async_computation.15 | async-start | bytes 3538944 | tf_op jit(solution)/shard_map/reduce_scatter | solution.py:244
  1049.6 222.0 %all-reduce.26.cloned.1.call-start = ((), (), s32[]{:S(2)}) async-start(), calls=%async_computation.19 | async-start | bytes 9568256
  1061.1 264.7 %reduce-scatter.17.cloned.1.call-start = ((), (), s32[]{:S(2)}) async-start(), calls=%async_computation.18 | async-start | bytes 4718592 | tf_op jit(solution)/shard_map/reduce_scatter | solution.py:247
  1070.1 311.2 %reduce-scatter.15.cloned.1.call-start = ((), (), s32[]{:S(2)}) async-start(), calls=%async_computation.17 | async-start | bytes 4718592 | tf_op jit(solution)/shard_map/reduce_scatter | solution.py:246
  1079.3 341.6 %reduce-scatter.13.cloned.1.call-start = ((), (), s32[]{:S(2)}) async-start(), calls=%async_computation.16 | async-start | bytes 1179648 | tf_op jit(solution)/shard_map/reduce_scatter | solution.py:245
  1086.2 185.4 %copy-start.4 = (f32[146,1,1024]{2,1,0:T(1,128)S(1)}, f32[146,1,1024]{2,1,0:T(1,128)}, u32[]{:S(2)}) copy-start(f32[146,1,1024]{2,1,0:T(1,128)} %copy-done.3) | copy-start | bytes 1794052
  1086.2 185.4 %copy-start.6 = (f32[146,1,1024]{2,1,0:T(1,128)S(1)}, f32[146,1,1024]{2,1,0:T(1,128)}, u32[]{:S(2)}) copy-start(f32[146,1,1024]{2,1,0:T(1,128)} %copy-done.5) | copy-start | bytes 1794052
  1086.2 185.4 %copy-start.39 = (f32[8,1,128]{2,1,0:T(1,128)S(1)}, f32[8,1,128]{2,1,0:T(1,128)}, u32[]{:S(2)}) copy-start(f32[8,1,128]{2,1,0:T(1,128)} %copy-done.38) | copy-start | bytes 12292
  1086.2 185.4 %copy-start.42 = (f32[146]{0:T(256)S(1)}, f32[146]{0:T(256)}, u32[]{:S(2)}) copy-start(f32[146]{0:T(256)} %copy-done.41) | copy-start | bytes 1756
  1086.2 185.4 %copy-start.44 = (f32[146]{0:T(256)S(1)}, f32[146]{0:T(256)}, u32[]{:S(2)}) copy-start(f32[146]{0:T(256)} %copy-done.43) | copy-start | bytes 1756
  1087.9 188.8 %copy-start.49 = (f32[146]{0:T(256)S(1)}, f32[146]{0:T(256)}, u32[]{:S(2)}) copy-start(f32[146]{0:T(256)} %copy-done.48) | copy-start | bytes 1756
  1087.9 188.8 %copy-start.47 = (f32[146]{0:T(256)S(1)}, f32[146]{0:T(256)}, u32[]{:S(2)}) copy-start(f32[146]{0:T(256)} %copy-done.46) | copy-start | bytes 1756
  (57 other events, 322.2 us)
Sparse Core Ops, SparseCore 0:
  37.9 51.3 all-gather.27
  91.2 24.4 all-gather.19
  117.8 51.0 all-gather.17
  199.0 173.2 all-reduce.29
  374.2 26.8 all-gather.23
  402.6 51.0 all-gather.29
  455.9 49.8 all-gather.21
  507.8 26.9 all-gather.25
  626.3 48.8 all-gather.31
  676.6 49.8 all-gather.35
  739.1 173.2 all-reduce.27
  925.7 50.0 all-gather.33
  977.8 49.8 all-gather.37
  1049.7 45.0 reduce-scatter.10
  1097.2 174.4 all-reduce.25
  1275.4 50.3 reduce-scatter.16
  1329.9 51.3 reduce-scatter.14
  1384.9 35.9 reduce-scatter.12
where the time goes:
time: 1430 us
  waiting for transfers between devices  1020 us (71%)
  blocking collectives  146 us (10%)
  matrix products  110 us (8%)
  other arithmetic  69.8 us (5%)
  local copies, waits for them, and re-layouts  58.6 us (4%)
  between operations  18.3 us (1%)
    unnamed x23, waiting for transfers between devices  498 us
    all_gather x2, waiting for transfers between devices, per_device(): normed2_all = lax.all_gather(normed2, 'tensor', axis=0, tiled=True)  99.5 us
    all_gather x2, waiting for transfers between devices, per_device(): normed_all = lax.all_gather(normed, 'tensor', axis=0, tiled=True)  89.8 us
    all_gather x2, waiting for transfers between devices, per_device(): mlp_grad_all = lax.all_gather(mlp_grad, 'tensor', axis=0, tiled=True)  86.1 us
    all_gather x2, waiting for transfers between devices, per_device(): branch_all = lax.all_gather(branch_grad, 'tensor', axis=0, tiled=True)  83.5 us
    unnamed x2, blocking collectives  73.4 us
    reduce_scatter x1, waiting for transfers between devices, per_device(): lax.psum_scatter(acc_up, 'dp', scatter_dimension=0, tiled=True)  55.5 us
    reduce_scatter x1, waiting for transfers between devices, per_device(): lax.psum_scatter(acc_proj, 'dp', scatter_dimension=1, tiled=True)  39.6 us
  transfers between devices with their start and end apart: 20, of which 18 were waited for; matrix products, arithmetic and copies ran while one was open for 9% of the time, Pallas kernels for 0%

commit v1 on v0

--- a/solution.py
+++ b/solution.py
@@ -1,6 +1,10 @@
+import functools
+
 import jax
 import jax.numpy as jnp
 from jax import lax
+from jax.experimental import pallas as pl
+from jax.experimental.pallas import tpu as pltpu
 from jax.sharding import PartitionSpec as P
 
 D = 1024
@@ -23,7 +27,7 @@
     return jax.nn.gelu(values, approximate=False)
 
 
-def per_device(
+def per_device_general(
     activations,
     cotangent,
     token_valid,
@@ -272,8 +276,841 @@
         owned[9],
     )
 
+MESH = pl.DeviceIdType.MESH
+F32 = jnp.float32
+BF16 = jnp.bfloat16
+TILES = 12
+T = 4
+NP = 4
+ROWS = D // (2 * NP)
+COLS = D // T
+VROWS = 32
+
+
+def place():
+    d = lax.axis_index("dp")
+    t = lax.axis_index("tensor")
+    c = lax.rem(d, 2)
+    p = d // 2
+    px = p + 1 - 2 * lax.rem(p, 2)
+    py = p + 2 - 4 * (p // 2)
+    return d, t, c, p, px, py, 3 - p
+
+
+def greet(d, t, c, p, px, py):
+    barrier = pltpu.get_barrier_semaphore()
+    me = c * T + t
+    for step in range(1, 2 * T):
+        other = lax.rem(me + step, 2 * T)
+        pl.semaphore_signal(
+            barrier, inc=1, device_id=(2 * p + other // T, lax.rem(other, T)), device_id_type=MESH
+        )
+    for q in (px, py):
+        pl.semaphore_signal(barrier, inc=1, device_id=(2 * q + c, t), device_id_type=MESH)
+    pl.semaphore_wait(barrier, 2 * T + 1)
+
+
+def remote(src, dst, send, recv, device):
+    return pltpu.make_async_remote_copy(
+        src_ref=src,
+        dst_ref=dst,
+        send_sem=send,
+        recv_sem=recv,
+        device_id=device,
+        device_id_type=MESH,
+    )
+
+
+class Exchange:
+    def __init__(self, src, dst, send, recv, spot, full):
+        d, t, c, p, px, py, pd = spot
+        self.c, self.t, self.p = c, t, p
+        self.src, self.dst, self.send, self.recv = src, dst, send, recv
+        self.full = full
+
+    def slot_out(self):
+        return self.t if self.full else lax.rem(self.t, 2)
+
+    def slot_in(self, k):
+        return 2 * self.c + k if self.full else k
+
+    def mine(self, k):
+        return jnp.logical_and(self.t // 2 == self.c, lax.rem(self.t, 2) == k)
+
+    def copy(self, k):
+        return remote(
+            self.src.at[k],
+            self.dst.at[self.slot_out()],
+            self.send.at[k],
+            self.recv.at[lax.rem(self.t, 2)],
+            (2 * self.p + self.t // 2, 2 * self.c + k),
+        )
+
+    def local(self, k):
+        return pltpu.make_async_copy(
+            self.src.at[k], self.dst.at[self.slot_out()], self.send.at[k]
+        )
+
+    def start(self):
+        for k in range(2):
+
+            @pl.when(self.mine(k))
+            def _():
+                self.local(k).start()
+
+            @pl.when(jnp.logical_not(self.mine(k)))
+            def _():
+                self.copy(k).start()
+
+    def wait_in(self, k):
+        @pl.when(self.mine(k))
+        def _():
+            self.local(k).wait()
+
+        @pl.when(jnp.logical_not(self.mine(k)))
+        def _():
+            remote(
+                self.src.at[k],
+                self.dst.at[self.slot_in(k)],
+                self.send.at[k],
+                self.recv.at[k],
+                (2 * self.p + self.t // 2, 2 * self.c + k),
+            ).wait_recv()
+
+    def wait_out(self, k):
+        @pl.when(jnp.logical_not(self.mine(k)))
+        def _():
+            self.copy(k).wait_send()
+
+
+class Gather:
+    def __init__(self, src, dst, sems, j, spot):
+        self.d, self.t, self.c, self.p, self.px, self.py, self.pd = spot
+        self.src, self.dst, self.j = src, dst, j
+        self.zin, self.zout, self.own_sem, self.rin, self.rout, self.cin, self.cout = sems
+        self.half = src.shape[0] // 2
+        self.width = src.shape[1]
+
+    def row(self, q):
+        return self.dst.at[q, self.c]
+
+    def cell(self, tau):
+        start = pl.multiple_of(tau * self.width, self.width)
+        return self.dst.at[self.p, self.c, :, pl.ds(start, self.width)]
+
+    def local(self):
+        return pltpu.make_async_copy(self.src, self.cell(self.t), self.own_sem.at[self.j])
+
+    def line(self, tau, way, k):
+        src = self.src if k == 0 else self.cell(tau)
+        return remote(
+            src,
+            self.cell(tau),
+            self.zout.at[self.j, way, k],
+            self.zin.at[self.j, tau],
+            (self.d, self.t + (1 if way == 0 else -1)),
+        )
+
+    def own(self):
+        self.local().start()
+
+        @pl.when(self.t < T - 1)
+        def _():
+            self.line(self.t, 0, 0).start()
+
+        @pl.when(self.t > 0)
+        def _():
+            self.line(self.t, 1, 0).start()
+
+    def hop(self, k):
+        t = self.t
+
+        @pl.when(t >= k)
+        def _():
+            self.line(t - k, 0, k).wait_recv()
+
+            @pl.when(t < T - 1)
+            def _():
+                self.line(t - k, 0, k).start()
+
+        @pl.when(t + k < T)
+        def _():
+            self.line(t + k, 1, k).wait_recv()
+
+            @pl.when(t > 0)
+            def _():
+                self.line(t + k, 1, k).start()
+
+    def side(self, way):
+        q = self.px if way == 0 else self.py
+        return (2 * q + self.c, self.t)
+
+    def near(self, way):
+        return remote(
+            self.row(self.p),
+            self.row(self.p),
+            self.rout.at[self.j, way],
+            self.rin.at[self.j, way],
+            self.side(way),
+        )
+
+    def near_in(self, way):
+        q = self.px if way == 0 else self.py
+        return remote(
+            self.row(q), self.row(q), self.rout.at[self.j, way], self.rin.at[self.j, way], self.side(way)
+        )
+
+    def far(self, way):
+        q = self.px if way == 0 else self.py
+        part = self.row(q).at[pl.ds(way * self.half, self.half)]
+        return remote(
+            part, part, self.rout.at[self.j, 2 + way], self.rin.at[self.j, 2 + way], self.side(1 - way)
+        )
+
+    def far_in(self, way):
+        part = self.row(self.pd).at[pl.ds(way * self.half, self.half)]
+        return remote(
+            part, part, self.rout.at[self.j, 2 + way], self.rin.at[self.j, 2 + way], self.side(1 - way)
+        )
+
+    def ring_one(self):
+        self.local().wait()
+        self.near(0).start()
+        self.near(1).start()
+
+    def ring_two(self):
+        for way in range(2):
+            self.near_in(way).wait_recv()
+            self.far(way).start()
+
+    def pair(self, c):
+        return remote(
+            self.dst.at[:, c],
+            self.dst.at[:, c],
+            self.cout.at[self.j],
+            self.cin.at[self.j],
+            (2 * self.p + 1 - self.c, self.t),
+        )
+
+    def ring_three(self):
+        for way in range(2):
+            self.far_in(way).wait_recv()
+        self.pair(self.c).start()
+
+    def finish(self):
+        self.pair(1 - self.c).wait_recv()
+        t = self.t
+        for k in range(T):
+
+            @pl.when(jnp.logical_and(t >= k, t < T - 1))
+            def _():
+                self.line(t - k, 0, k).wait_send()
+
+            @pl.when(jnp.logical_and(t + k < T, t > 0))
+            def _():
+                self.line(t + k, 1, k).wait_send()
+
+        for way in range(2):
+            self.near(way).wait_send()
+            self.far(way).wait_send()
+        self.pair(self.c).wait_send()
+
+
+def gather_kernel(
+    w, v, x, cot, valid, full_w, full_v, full_x, full_cot, full_valid, *sems
+):
+    ex_sem, mask_sem, pass_sem, chunk_sems = sems[0], sems[1], sems[2], sems[3:]
+    spot = place()
+    d, t, c, p, px, py, pd = spot
+    greet(d, t, c, p, px, py)
+    partner = (2 * p + 1 - c, t)
+    swap_x = Exchange(x, full_x, ex_sem.at[0], ex_sem.at[1], spot, True)
+    swap_c = Exchange(cot, full_cot, ex_sem.at[2], ex_sem.at[3], spot, False)
+    swap_x.start()
+    mask_out = remote(valid, full_valid.at[c], mask_sem.at[0], mask_sem.at[1], partner)
+    mask_in = remote(valid, full_valid.at[1 - c], mask_sem.at[0], mask_sem.at[1], partner)
+    mask_own = pltpu.make_async_copy(valid, full_valid.at[c], mask_sem.at[2])
+    mask_out.start()
+    mask_own.start()
+
+    def passed(core, k):
+        view = full_x.at[2 * core + k]
+        return remote(view, view, pass_sem.at[0, k], pass_sem.at[1, k], partner)
+
+    chunks = [Gather(v, full_v, chunk_sems, 0, spot)]
+    for j in range(TILES):
+        chunks.append(Gather(w.at[j], full_w.at[j], chunk_sems, j + 1, spot))
+    count = len(chunks)
+    for s in range(count + 6):
+        for lag, stage in (
+            (5, lambda g: g.ring_three()),
+            (4, lambda g: g.ring_two()),
+            (3, lambda g: (g.hop(3), g.ring_one())),
+            (2, lambda g: g.hop(2)),
+            (1, lambda g: g.hop(1)),
+            (0, lambda g: g.own()),
+        ):
+            if 0 <= s - lag < count:
+                stage(chunks[s - lag])
+        if s == 0:
+            swap_c.start()
+        if s == 3:
+            for k in range(2):
+                swap_x.wait_in(k)
+                passed(c, k).start()
+    for k in range(2):
+        swap_c.wait_in(k)
+        passed(1 - c, k).wait_recv()
+    mask_in.wait_recv()
+    mask_own.wait()
+    for chunk in chunks:
+        chunk.finish()
+    for k in range(2):
+        passed(c, k).wait_send()
+        swap_x.wait_out(k)
+        swap_c.wait_out(k)
+    mask_out.wait_send()
+
+
+def gather_all(w, v, x, cot, valid):
+    any_space = pl.BlockSpec(memory_space=pl.ANY)
+    dma = pltpu.SemaphoreType.DMA
+    n = TILES + 1
+    lead = NP, 2
+    return pl.pallas_call(
+        gather_kernel,
+        out_shape=(
+            jax.ShapeDtypeStruct((TILES,) + lead + (ROWS, D), BF16),
+            jax.ShapeDtypeStruct(lead + (VROWS, 128 * T), BF16),
+            jax.ShapeDtypeStruct((T,) + x.shape[1:], BF16),
+            jax.ShapeDtypeStruct(cot.shape, BF16),
+            jax.ShapeDtypeStruct((2,) + valid.shape, F32),
+        ),
+        in_specs=[any_space] * 5,
+        out_specs=[any_space] * 5,
+        scratch_shapes=[
+            dma((4, 2)),
+            dma((3,)),
+            dma((2, 2)),
+            dma((n, T)),
+            dma((n, 2, T)),
+            dma((n,)),
+            dma((n, 4)),
+            dma((n, 4)),
+            dma((n,)),
+            dma((n,)),
+        ],
+        name="gather_all",
+        compiler_params=pltpu.CompilerParams(collective_id=0, has_side_effects=True, vmem_limit_bytes=8 << 20),
+    )(w, v, x, cot, valid)
+
+
+def scatter_kernel(
+    at, b, vec, blk, ig, out, vec_out, own_blk, own_ig,
+    stage, held, far_in, near_in, line_in, vec_held, vec_in,
+    pair_out, pair_in, far_sem, near_sem, line_sem, vec_sem, ex_sem,
+):
+    spot = place()
+    d, t, c, p, px, py, pd = spot
+    greet(d, t, c, p, px, py)
+    partner = (2 * p + 1 - c, t)
+    side = ((2 * px + c, t), (2 * py + c, t))
+    swap_b = Exchange(blk, own_blk, ex_sem.at[0], ex_sem.at[1], spot, False)
+    swap_i = Exchange(ig, own_ig, ex_sem.at[2], ex_sem.at[3], spot, False)
+    half = ROWS // 2
+
+    def pair(j):
+        return remote(
+            stage.at[lax.rem(j, 2)], held.at[j], pair_out.at[lax.rem(j, 2)], pair_in.at[j], partner
+        )
+
+    def far(j, way):
+        return remote(
+            held.at[j, pd, pl.ds(way * half, half)],
+            far_in.at[j, way],
+            far_sem.at[0, j, way],
+            far_sem.at[1, j, way],
+            side[way],
+        )
+
+    def near(j, way):
+        return remote(
+            held.at[j, (px, py)[way]],
+            near_in.at[j, way],
+            near_sem.at[0, j, way],
+            near_sem.at[1, j, way],
+            side[way],
+        )
+
+    def line(j, tau, way):
+        return remote(
+            held.at[j, p, :, pl.ds(tau * COLS, COLS)],
+            line_in.at[j, way, tau],
+            line_sem.at[0, j, way, tau],
+            line_sem.at[1, j, way, tau],
+            (d, t + (1 if way == 0 else -1)),
+        )
+
+    vec_partners = (
+        partner,
+        side[0],
+        side[1],
+        (d, t + 1 - 2 * lax.rem(t, 2)),
+        (d, t + 2 - 4 * (t // 2)),
+    )
+
+    def vec_copy(r):
+        return remote(vec_held.at[r], vec_in.at[r], vec_sem.at[0, r], vec_sem.at[1, r], vec_partners[r])
+
+    def product(j, q, core):
+        kind = (j + 4) // 4 - (14 - j) // 12
+        rows = pl.ds(pl.multiple_of((2 * q + core) * ROWS, ROWS), ROWS)
+        return jnp.dot(at[kind, rows], b[j], preferred_element_type=F32)
+
+    vec_held[0] = vec[...]
+    vec_copy(0).start()
+    swap_b.start()
+    swap_i.start()
+
+    def step(s, carry):
+        for r in range(5):
+
+            @pl.when(s == 2 * r + 1)
+            def _():
+                vec_copy(r).wait_recv()
+                vec_held[r + 1] = vec_held[r] + vec_in[r]
+                if r < 4:
+                    vec_copy(r + 1).start()
+
+        @pl.when(s < TILES)
+        def _():
+            @pl.when(s >= 2)
+            def _():
+                pair(s - 2).wait_send()
+
+            slot = lax.rem(s, 2)
+            for q in range(NP):
+                stage[slot, q] = product(s, q, 1 - c).astype(BF16)
+            pair(s).start()
+
+        @pl.when(jnp.logical_and(s >= 1, s < TILES + 1))
+        def _():
+            j = s - 1
+            pair(j).wait_recv()
+            for q in range(NP):
+                held[j, q] = (product(j, q, c) + held[j, q].astype(F32)).astype(BF16)
+            for way in range(2):
+                far(j, way).start()
+
+        @pl.when(jnp.logical_and(s >= 2, s < TILES + 2))
+        def _():
+            j = s - 2
+            for way in range(2):
+                far(j, way).wait_recv()
+                part = pl.ds(way * half, half)
+                q = (py, px)[way]
+                held[j, q, part] = (
+                    held[j, q, part].astype(F32) + far_in[j, way].astype(F32)
+                ).astype(BF16)
+                near(j, 1 - way).start()
+
+        @pl.when(jnp.logical_and(s >= 3, s < TILES + 3))
+        def _():
+            j = s - 3
+            near(j, 0).wait_recv()
+            near(j, 1).wait_recv()
+            for tau in range(T):
+                cols = pl.ds(tau * COLS, COLS)
+                total = (
+                    held[j, p, :, cols].astype(F32)
+                    + near_in[j, 0, :, cols].astype(F32)
+                    + near_in[j, 1, :, cols].astype(F32)
+                )
+                held[j, p, :, cols] = total.astype(BF16)
+
+                @pl.when(t == tau)
+                def _():
+                    out[j] = total
+
+        for way in range(2):
+            hop = t if way == 0 else T - 1 - t
+            j = s - 4 - hop
+
+            @pl.when(jnp.logical_and(j >= 0, j < TILES))
+            def _():
+                for tau in range(T):
+
+                    @pl.when((tau > t) if way == 0 else (tau < t))
+                    def _():
+                        cols = pl.ds(tau * COLS, COLS)
+
+                        @pl.when(hop > 0)
+                        def _():
+                            line(j, tau, way).wait_recv()
+                            held[j, p, :, cols] = (
+                                held[j, p, :, cols].astype(F32) + line_in[j, way, tau].astype(F32)
+                            ).astype(BF16)
+
+                        line(j, tau, way).start()
+
+        @pl.when(s >= 8)
+        def _():
+            j = s - 8
+            for way in range(2):
+
+                @pl.when((t > 0) if way == 0 else (t < T - 1))
+                def _():
+                    for tau in range(T):
+
+                        @pl.when(t == tau)
+                        def _():
+                            line(j, tau, way).wait_recv()
+                            out[j] += line_in[j, way, tau].astype(F32)
+
+        return carry
+
+    lax.fori_loop(0, TILES + 8, step, 0)
+
+    def drain(j, carry):
+        for way in range(2):
+            far(j, way).wait_send()
+            near(j, way).wait_send()
+            for tau in range(T):
+
+                @pl.when((tau > t) if way == 0 else (tau < t))
+                def _():
+                    line(j, tau, way).wait_send()
+
+        return carry
+
+    lax.fori_loop(0, TILES, drain, 0)
+    pair(TILES - 2).wait_send()
+    pair(TILES - 1).wait_send()
+    vec_out[...] = vec_held[5]
+    for r in range(5):
+        vec_copy(r).wait_send()
+    for swap in (swap_b, swap_i):
+        for k in range(2):
+            swap.wait_in(k)
+            swap.wait_out(k)
+
+
+def scatter_all(at, b, vec, blk, ig):
+    any_space = pl.BlockSpec(memory_space=pl.ANY)
+    vmem = pl.BlockSpec(memory_space=pltpu.VMEM)
+    dma = pltpu.SemaphoreType.DMA
+    n = TILES
+    return pl.pallas_call(
+        scatter_kernel,
+        out_shape=(
+            jax.ShapeDtypeStruct((n, ROWS, COLS), F32),
+            jax.ShapeDtypeStruct(vec.shape, F32),
+            jax.ShapeDtypeStruct(blk.shape, BF16),
+            jax.ShapeDtypeStruct(ig.shape, BF16),
+        ),
+        in_specs=[vmem, vmem, vmem, any_space, any_space],
+        out_specs=[vmem, vmem, any_space, any_space],
+        scratch_shapes=[
+            pltpu.VMEM((2, NP, ROWS, D), BF16),
+            pltpu.VMEM((n, NP, ROWS, D), BF16),
+            pltpu.VMEM((n, 2, ROWS // 2, D), BF16),
+            pltpu.VMEM((n, 2, ROWS, D), BF16),
+            pltpu.VMEM((n, 2, T, ROWS, COLS), BF16),
+            pltpu.VMEM((6,) + vec.shape, F32),
+            pltpu.VMEM((5,) + vec.shape, F32),
+            dma((2,)),
+            dma((n,)),
+            dma((2, n, 2)),
+            dma((2, n, 2)),
+            dma((2, n, 2, T)),
+            dma((2, 5)),
+            dma((4, 2)),
+        ],
+        name="scatter_all",
+        compiler_params=pltpu.CompilerParams(
+            collective_id=1, has_side_effects=True, vmem_limit_bytes=58 << 20
+        ),
+    )(at, b, vec, blk, ig)
+
+
+def head_probs(k, q_t, bias):
+    s = jnp.dot(k, q_t, preferred_element_type=F32) + bias
+    e = jnp.exp(s - jnp.max(s, axis=0, keepdims=True))
+    return e / jnp.sum(e, axis=0, keepdims=True)
+
+
+def head_rows(q_t, h):
+    row = lax.broadcasted_iota(jnp.int32, q_t.shape, 0) // HD
+    return jnp.where(row == h, q_t, jnp.zeros_like(q_t))
+
+
+def head_lanes(q, h):
+    lane = lax.broadcasted_iota(jnp.int32, q.shape, 1) // HD
+    return jnp.where(lane == h, q, jnp.zeros_like(q))
+
+
+def attend_kernel(q, k, v, bias, out):
+    q_t = (q[...].astype(F32).T * HD ** (-0.5)).astype(BF16)
+    v_t = v[...].astype(F32).T.astype(BF16)
+    parts = []
+    for h in range(2):
+        probs = head_probs(k[...], head_rows(q_t, h), bias[...]).astype(BF16)
+        parts.append(
+            jnp.dot(v_t[h * HD : (h + 1) * HD], probs, preferred_element_type=F32)
+        )
+    out[...] = jnp.concatenate(parts, axis=0).T.astype(BF16)
+
+
+def attend_back_kernel(q, k, v, g, bias, dq, dk, dv):
+    q_s = (q[...].astype(F32) * HD ** (-0.5)).astype(BF16)
+    q_t = q_s.astype(F32).T.astype(BF16)
+    g_t = g[...].astype(F32).T.astype(BF16)
+    k_t = k[...].astype(F32).T.astype(BF16)
+    parts = []
+    dk_sum = jnp.zeros(dk.shape, F32)
+    dv_sum = jnp.zeros(dv.shape, F32)
+    for h in range(2):
+        probs = head_probs(k[...], head_rows(q_t, h), bias[...])
+        dv_sum += jnp.dot(probs.astype(BF16), head_lanes(g[...], h), preferred_element_type=F32)
+        dp = jnp.dot(v[...], head_rows(g_t, h), preferred_element_type=F32)
+        ds = (probs * (dp - jnp.sum(dp * probs, axis=0, keepdims=True))).astype(BF16)
+        parts.append(jnp.dot(k_t[h * HD : (h + 1) * HD], ds, preferred_element_type=F32))
+        dk_sum += jnp.dot(ds, head_lanes(q_s, h), preferred_element_type=F32)
+    dq[...] = (jnp.concatenate(parts, axis=0).T * HD ** (-0.5)).astype(BF16)
+    dk[...] = dk_sum.astype(dk.dtype)
+    dv[...] = dv_sum.astype(dv.dtype)
+
+
+def columns(rows):
+    return pl.BlockSpec((rows, 2 * HD), lambda i: (0, i))
+
+
+def attend(q, k, v, bias):
+    nq, nk = q.shape[0], k.shape[0]
+    return pl.pallas_call(
+        attend_kernel,
+        grid=(H // 2,),
+        out_shape=jax.ShapeDtypeStruct((nq, D), BF16),
+        in_specs=[columns(nq), columns(nk), columns(nk), pl.BlockSpec((nk, 1), lambda i: (0, 0))],
+        out_specs=columns(nq),
+        name="attend",
+        compiler_params=pltpu.CompilerParams(vmem_limit_bytes=48 << 20),
+    )(q, k, v, bias)
+
+
+def attend_back(q, k, v, g, bias):
+    nq, nk = q.shape[0], k.shape[0]
+    return pl.pallas_call(
+        attend_back_kernel,
+        grid=(H // 2,),
+        out_shape=(
+            jax.ShapeDtypeStruct((nq, D), BF16),
+            jax.ShapeDtypeStruct((nk, D), BF16),
+            jax.ShapeDtypeStruct((nk, D), BF16),
+        ),
+        in_specs=[
+            columns(nq),
+            columns(nk),
+            columns(nk),
+            columns(nq),
+            pl.BlockSpec((nk, 1), lambda i: (0, 0)),
+        ],
+        out_specs=(columns(nq), columns(nk), columns(nk)),
+        name="attend_back",
+        compiler_params=pltpu.CompilerParams(vmem_limit_bytes=48 << 20),
+    )(q, k, v, g, bias)
+
+
+def norm_parts(values):
+    center = values - jnp.mean(values, axis=-1, keepdims=True)
+    spread = jnp.mean(center * center, axis=-1, keepdims=True)
+    inverse = lax.rsqrt(spread + EPS)
+    return center * inverse, inverse
+
+
+def norm_back(grad, unit, inverse, gain):
+    scaled = grad * gain
+    return inverse * (
+        scaled
+        - jnp.mean(scaled, axis=-1, keepdims=True)
+        - unit * jnp.mean(scaled * unit, axis=-1, keepdims=True)
+    )
+
+
+def dot_nn(a, b):
+    return lax.dot_general(a, b, (((1,), (0,)), ((), ())), preferred_element_type=F32)
+
+
+def dot_nt(a, b):
+    return lax.dot_general(a, b, (((1,), (1,)), ((), ())), preferred_element_type=F32)
+
+
+def per_device_chips(
+    activations, cotangent, token_valid, image_counts, pre_gain, pre_shift, attn_weight,
+    attn_bias, proj_weight, proj_bias, mid_gain, mid_shift, up_weight, up_bias, down_weight,
+    down_bias,
+):
+    local_rows = activations.shape[0]
+    slots = activations.shape[1]
+    block = -(-local_rows // 16) * 16
+    pad = block - local_rows
+    d = lax.axis_index("dp")
+    t = lax.axis_index("tensor")
+    c = lax.rem(d, 2)
+    first_row = t * local_rows
+    my_valid = lax.dynamic_slice_in_dim(token_valid, first_row, local_rows, 1).astype(F32)
+    slot_live = (jnp.arange(slots, dtype=jnp.int32) < image_counts[0]).astype(F32)
+    out_mask = jnp.transpose(slot_live[:, None] * my_valid)[:, :, None]
+
+    def to_blocks(a):
+        return jnp.pad(jnp.transpose(a, (1, 0, 2)), ((0, 0), (0, pad), (0, 0)))
+
+    x_blocks = to_blocks(activations)
+    c_blocks = to_blocks((cotangent.astype(F32) * out_mask).astype(BF16))
+    valid = jnp.pad(
+        token_valid.astype(F32).reshape(slots, T, local_rows), ((0, 0), (0, 0), (0, pad))
+    ).reshape(slots, T * block)
+    valid = jnp.pad(valid, ((0, 8 - slots), (0, 0)))
+    per_j = up_weight.shape[1] // COLS
+    w = jnp.concatenate(
+        [
+            attn_weight,
+            jnp.transpose(proj_weight)[None],
+            jnp.transpose(up_weight.reshape(ROWS, per_j, COLS), (1, 0, 2)),
+            jnp.transpose(down_weight.reshape(per_j, COLS, ROWS), (0, 2, 1)),
+        ],
+        axis=0,
+    )
+    v = jnp.concatenate(
+        [
+            jnp.stack([pre_gain, pre_shift, proj_bias, mid_gain, mid_shift, down_bias]),
+            attn_bias.reshape(-1, 128),
+            up_bias.reshape(-1, 128),
+        ],
+        axis=0,
+    )
+    v = jnp.pad(v, ((0, VROWS - v.shape[0]), (0, 0)))
+    full_w, full_v, full_x, own_cot, full_valid = gather_all(w, v, x_blocks, c_blocks, valid)
+    g = full_w.reshape(TILES, D, D)
+    vectors = full_v[:, :, :6, :128].astype(F32)
+    gain_one, shift_one, proj_b, gain_two, shift_two, down_b = [
+        vectors[:, :, i].reshape(1, D) for i in range(6)
+    ]
+    split = full_v[0, 0].reshape(VROWS, T, 128).astype(F32)
+    per_tau = COLS // 128
+
+    def spread_out(first, count):
+        part = split[first : first + count * per_tau].reshape(count, per_tau, T, 128)
+        return jnp.transpose(part, (0, 2, 1, 3)).reshape(count, 1, D)
+
+    attn_b = spread_out(6, 2)
+    up_b = spread_out(6 + 2 * per_tau, per_j)
+
+    nk = T * block
+    nq = nk // 2
+    x_all = full_x.reshape(nk, D).astype(F32)
+    image_valid = lax.dynamic_slice(
+        full_valid, (t // 2, lax.rem(t, 2), 0), (1, 1, nk)
+    ).reshape(nk, 1)
+    bias = jnp.where(image_valid > 0, 0.0, NEG).astype(F32)
+
+    def mine(a):
+        return lax.dynamic_slice_in_dim(a, c * nq, nq, 0)
+
+    def other(a):
+        return lax.dynamic_slice_in_dim(a, (1 - c) * nq, nq, 0)
+
+    unit_all, inverse_all = norm_parts(x_all)
+    normed_all = (unit_all * gain_one + shift_one).astype(BF16)
+    normed = mine(normed_all)
+    x_own = mine(x_all)
+    queries = (dot_nn(normed, g[0]) + attn_b[0]).astype(BF16)
+    keys = dot_nn(normed_all, g[1]).astype(BF16)
+    values = (dot_nn(normed_all, g[2]) + attn_b[1]).astype(BF16)
+    attended = attend(queries, keys, values, bias)
+    resid = x_own + dot_nt(attended, g[3]) + proj_b
+    unit_two, inverse_two = norm_parts(resid)
+    normed2 = (unit_two * gain_two + shift_two).astype(BF16)
+    mlp_grad = own_cot.reshape(nq, D)
+    outer = mlp_grad.astype(F32)
+    hidden, pre_grad, up_sums = [], [], []
+    mlp_out = jnp.zeros((nq, D), F32)
+    normed2_grad = jnp.zeros((nq, D), F32)
+    for j in range(per_j):
+        hidden_pre = dot_nn(normed2, g[4 + j]) + up_b[j]
+        act, back = jax.vjp(gelu_exact, hidden_pre)
+        act = act.astype(BF16)
+        hidden.append(act)
+        mlp_out = mlp_out + dot_nt(act, g[8 + j])
+        grad = back(dot_nn(mlp_grad, g[8 + j]))[0].astype(BF16)
+        pre_grad.append(grad)
+        up_sums.append(jnp.sum(grad.astype(F32), axis=0))
+        normed2_grad = normed2_grad + dot_nt(grad, g[4 + j])
+    block_own = (resid + mlp_out + down_b).astype(BF16)
+    resid_grad = outer + norm_back(normed2_grad, unit_two, inverse_two, gain_two)
+    branch = resid_grad.astype(BF16)
+    att_grad = dot_nn(branch, g[3]).astype(BF16)
+    dq, dk, dv = attend_back(queries, keys, values, att_grad, bias)
+    swap = [(i, i + 1 - 2 * (i % 2)) for i in range(2 * NP)]
+    dkv = jnp.concatenate([dk, dv], axis=1)
+    came = lax.ppermute(other(dkv), "dp", swap)
+    dkv = (mine(dkv).astype(F32) + came.astype(F32)).astype(BF16)
+    dk, dv = dkv[:, :D], dkv[:, D:]
+    normed_grad = dot_nt(dq, g[0]) + dot_nt(dk, g[1]) + dot_nt(dv, g[2])
+    unit_one, inverse_one = mine(unit_all), mine(inverse_all)
+    input_own = resid_grad + norm_back(normed_grad, unit_one, inverse_one, gain_one)
+    sums = jnp.stack(
+        [
+            jnp.sum(normed_grad * unit_one, axis=0),
+            jnp.sum(normed_grad, axis=0),
+            jnp.sum(branch.astype(F32), axis=0),
+            jnp.sum(normed2_grad * unit_two, axis=0),
+            jnp.sum(normed2_grad, axis=0),
+            jnp.sum(outer, axis=0),
+            jnp.sum(dq.astype(F32), axis=0),
+            jnp.sum(dv.astype(F32), axis=0),
+        ]
+        + up_sums
+    )
+    at = jnp.stack([jnp.transpose(a) for a in (normed, branch, normed2, mlp_grad)])
+    b = jnp.stack([dq, dk, dv, attended] + pre_grad + hidden)
+    grads, totals, own_block, own_input = scatter_all(
+        at,
+        b,
+        sums.reshape(-1, 128),
+        block_own.reshape(2, block, D),
+        input_own.astype(BF16).reshape(2, block, D),
+    )
+    totals = totals.reshape(-1, D)
+    owned = lax.dynamic_slice(totals, (0, d * ROWS), (6, ROWS))
+    parted = lax.dynamic_slice(totals, (0, t * COLS), (totals.shape[0], COLS))
+
+    def from_blocks(a):
+        return jnp.transpose(a[:, :local_rows], (1, 0, 2))
+
+    block_out = (from_blocks(own_block).astype(F32) * out_mask).astype(BF16)
+    input_grad = from_blocks(own_input).astype(F32)
+    return (
+        block_out,
+        input_grad,
+        owned[0],
+        owned[1],
+        grads[0:3],
+        parted[6:8],
+        jnp.transpose(grads[3]),
+        owned[2],
+        owned[3],
+        owned[4],
+        jnp.transpose(grads[4 : 4 + per_j], (1, 0, 2)).reshape(ROWS, per_j * COLS),
+        parted[8 : 8 + per_j].reshape(-1),
+        jnp.transpose(grads[4 + per_j :], (0, 2, 1)).reshape(per_j * COLS, ROWS),
+        owned[5],
+    )
+
 
 def solution(mesh):
+    sizes = (mesh.shape["dp"], mesh.shape["tensor"])
+    per_device = per_device_chips if sizes == (2 * NP, T) else per_device_general
     return jax.shard_map(
         per_device,
         mesh=mesh,

time: 1430 us -> 490 us (0.34)
  waiting for transfers between devices: 1020 us -> 0.01 us
  Pallas kernels: 0 us -> 334 us
  blocking collectives: 146 us -> 0 us
  matrix products: 110 us -> 45.4 us
  other arithmetic: 69.8 us -> 18.7 us
  local copies, waits for them, and re-layouts: 58.6 us -> 83.6 us
  between operations: 18.3 us -> 2.54 us
    unnamed x23 -> x0, waiting for transfers between devices: 498 us -> none
    all_gather x11 -> x0, waiting for transfers between devices: 414 us -> none  [the longest x2 99.5 us: per_device(): normed2_all = lax.all_gather(normed2, 'tensor', axis=0, tiled=True)]
    pallas_call x0 -> x4, Pallas kernels: none -> 334 us  [the longest x1 164 us: gather_all(): pl.pallas_call(gather_kernel, out_shape=(jax.ShapeDtypeStruct((TILES,) +...]
    reduce_scatter x4 -> x0, waiting for transfers between devices: 106 us -> none  [the longest x1 55.5 us: per_device(): lax.psum_scatter(acc_up, 'dp', scatter_dimension=0, tiled=True)]
    unnamed x2 -> x0, blocking collectives: 73.4 us -> none
    dot_general x36 -> x24, matrix products: 110 us -> 45.4 us  [the longest x12 28.5 us: dot_nn(): lax.dot_general(a, b, (((1,), (0,)), ((), ())), preferred_element_type=F32)]
    all_gather x7 -> x0, blocking collectives: 62.4 us -> none  [the longest x1 10.3 us: per_device(): lax.all_gather(pre_gain, 'dp', axis=0, tiled=True)]
    reduce_sum x13 -> x7, other arithmetic: 42.2 us -> 2.02 us  [the longest x2 0.74 us: norm_parts(): spread = jnp.mean(center * center, axis=-1, keepdims=True)]
  transfers between devices with their start and end apart: 20 -> 1, of which waited for: 18 -> 0; matrix products, arithmetic and copies ran while one was open for 9% -> 1% of each run, Pallas kernels for 0% -> 0%
where the time goes in v1:
time: 490 us; the launch traced here: 484 us
  Pallas kernels  334 us (68%)
  local copies, waits for them, and re-layouts  83.6 us (17%)
  matrix products  45.4 us (9%)
  other arithmetic  18.7 us (4%)
    pallas_call x1, Pallas kernels, gather_all(): pl.pallas_call(gather_kernel, out_shape=(jax.ShapeDtypeStruct((TILES,) +...  164 us
    pallas_call x1, Pallas kernels, scatter_all(): pl.pallas_call(scatter_kernel, out_shape=(jax.ShapeDtypeStruct((n, ROWS,...  135 us
    unnamed x152, local copies, waits for them, and re-layouts  45.4 us
    dot_general x12, matrix products, dot_nn(): lax.dot_general(a, b, (((1,), (0,)), ((), ())), preferred_element_type=F32)  28.5 us
    pallas_call x1, Pallas kernels, attend_back(): pl.pallas_call(attend_back_kernel, grid=(H // 2,), out_shape=(jax.ShapeDt...  22.1 us
    slice x2, local copies, waits for them, and re-layouts, per_device_chips(): hidden_pre = dot_nn(normed2, g[4 + j]) + up_b[j]  17.5 us
    dot_general x12, matrix products, dot_nt(): lax.dot_general(a, b, (((1,), (1,)), ((), ())), preferred_element_type=F32)  16.9 us
    pallas_call x1, Pallas kernels, attend(): pl.pallas_call(attend_kernel, grid=(H // 2,), out_shape=jax.ShapeDtypeStr...  11.9 us
  transfers between devices with their start and end apart: 1, of which 0 were waited for; matrix products, arithmetic and copies ran while one was open for 1% of the time, Pallas kernels for 0%

profile of v1, /device:TPU:0, one launch (start us, length us, event | category | flops | bytes accessed | tf_op | source)
XLA Modules:
  0.0 484.4 jit_solution(9855109510029398614)
XLA Ops:
  7.9 164.3 %gather_all.1 = (bf16[12,4,2,128,1024]{4,3,2,1,0:T(8,128)(2,1)S(1)}, bf16[4,2,32,512]{3,2,1,0:T(8,128)(2,1)S(1)}, bf16[4,160,1024]{2,1,0:T(8,128)(2,1)S(1)}, bf1...) custom-call(bf16[12,128,256]{2,1,0:T(8,128)(2,1)S(1)} %pad_maximum_fusion.1.w, bf16[32,128]{1,0:T(8,128)(2,1)S(1)} %pad.19.v, ...), custom_call_target="tpu_custom_call" | custom-call | tf_op jit(solution)/shard_map/gather_all/pallas_call | solution.py:580
  172.2 8.3 %copy-done = bf16[12,4,2,128,1024]{4,3,2,1,0:T(8,128)(2,1)} copy-done((bf16[12,4,2,128,1024]{4,3,2,1,0:T(8,128)(2,1)}, bf16[12,4,2,128,1024]{4,3,2,1,0:T(8,128)(2,1)S(1)}, u32[]{:S(2)}) %copy-start) | copy-done | bytes 25165848
  181.4 17.5 %fusion.38 = (bf16[1,4,2,128,1024]{4,3,2,1,0:T(8,128)(2,1)}, bf16[1,4,2,128,1024]{4,3,2,1,0:T(8,128)(2,1)}, bf16[1,4,2,128,1024]{4,3,2,1,0:T(8,128)(2,1)}, bf16[...) fusion(bf16[12,4,2,128,1024]{4,3,2,1,0:T(8,128)(2,1)} %copy-done), kind=kLoop, calls=%fused_computation.164 | loop fusion | bytes 50331648 | tf_op jit(solution)/shard_map/slice | solution.py:1040
  200.5 1.8 copy.58
  203.9 1.5 convolution_convert_fusion.k
  205.5 1.5 add_convert_fusion.1.v
  207.5 2.8 copy-done.17
  210.3 1.9 fusion.q
  212.2 11.9 %attend.1 = bf16[320,1024]{1,0:T(8,128)(2,1)S(1)} custom-call(bf16[320,1024]{1,0:T(8,128)(2,1)S(1)} %fusion.q, bf16[640,1024]{1,0:T(8,128)(2,1)S(1)} %convolution_convert_fusion.k, bf16[640,1024]{1,0:T(8,128)(2,1)S(1)} %add_convert_fusion.1.v, f32[640,1]{1,0:T(8,128)S(1)} %copy.62.bias), custom_call_target="tpu_custom_call" | custom-call | tf_op jit(solution)/shard_map/attend/pallas_call | solution.py:890
  224.1 1.3 fusion.42
  226.0 1.5 copy-done.16
  229.2 4.9 %convert_reduce_fusion.5 = (f32[1024]{0:T(1024)S(1)}, bf16[320,1024]{1,0:T(8,128)(2,1)S(1)}, f32[320,1024]{1,0:T(8,128)}) fusion(f32[320,1024]{1,0:T(8,128)S(1)} %convolution_add_fusion.3, bf16[320,1024]{1,0:T(8,128)(2,1)S(1)} %bitcast.191, bf16[1024,1024]{1,0:T(8,128)(2,1)S(1)} %bitcast.219), kind=kOutput, calls=%fused_computation.43 | convolution fusion | flops 695335936 | bytes 6033408 | tf_op jit(solution)/shard_map/dot_general | solution.py:941
  237.5 4.7 convert_reduce_fusion.4
  245.6 4.6 convert_reduce_fusion.3
  250.2 1.3 fusion.45
  253.6 5.1 %convert_reduce_fusion.2 = (f32[1024]{0:T(1024)S(1)}, bf16[320,1024]{1,0:T(8,128)(2,1)S(1)}, f32[320,1024]{1,0:T(8,128)}) fusion(f32[320,1024]{1,0:T(8,128)S(1)} %convolution_add_fusion, bf16[320,1024]{1,0:T(8,128)(2,1)S(1)} %bitcast.194, bf16[1024,1024]{1,0:T(8,128)(2,1)S(1)} %bitcast.209), kind=kOutput, calls=%fused_computation.40 | convolution fusion | flops 695335936 | bytes 6033408 | tf_op jit(solution)/shard_map/dot_general | solution.py:941
  258.8 2.0 multiply_reduce_fusion.2
  263.6 22.1 %attend_back.1 = (bf16[320,1024]{1,0:T(8,128)(2,1)S(1)}, bf16[640,1024]{1,0:T(8,128)(2,1)S(1)}, bf16[640,1024]{1,0:T(8,128)(2,1)S(1)}) custom-call(bf16[320,1024]{1,0:T(8,128)(2,1)S(1)} %fusion.q, bf16[640,1024]{1,0:T(8,128)(2,1)S(1)} %convolution_convert_fusion.k, bf16[640,1024]{1,0:T(8,128)(2,1)} %copy-done.1, ...), custom_call_target="tpu_custom_call" | custom-call | tf_op jit(solution)/shard_map/attend_back/pallas_call | solution.py:903
  288.0 2.5 constant_dynamic-update-slice_fusion
  290.5 2.5 constant_dynamic-slice_fusion.2
  298.9 1.9 add_convert_fusion
  300.9 1.3 fusion.27
  303.3 1.8 multiply_reduce_fusion.1
  305.1 2.5 add_convert_fusion.3
  307.6 2.2 copy.79
  330.2 1.6 add_convert_fusion.4
  333.0 3.3 pad_maximum_fusion.at
  336.3 135.4 %scatter_all.1 = (f32[12,128,256]{2,1,0:T(8,128)}, f32[96,128]{1,0:T(8,128)}, bf16[2,160,1024]{2,1,0:T(8,128)(2,1)}, bf16[2,160,1024]{2,1,0:T(8,128)(2,1)}) custom-call(bf16[4,1024,320]{2,1,0:T(8,128)(2,1)} %pad_maximum_fusion.at, bf16[12,320,1024]{2,1,0:T(8,128)(2,1)} %get-tuple-element.88.b, f32[96,128]{1,0:T(8,128)} %reshape.289.vec, ...), custom_call_target="tpu_custom_call" | custom-call | tf_op jit(solution)/shard_map/scatter_all/pallas_call | solution.py:803
  472.6 1.8 slice.198
  474.4 1.3 slice_bitcast_fusion
  475.9 1.4 copy.82
  482.3 1.9 copy.83
  (228 shorter events, 61.2 us)
Async XLA Ops:
  0.6 4.7 copy-start.57
  0.7 5.7 %copy-start.66 = (bf16[128]{0:T(256)(128)(2,1)S(1)}, bf16[128]{0:T(256)(128)(2,1)}, u32[]{:S(2)}) copy-start(bf16[128]{0:T(256)(128)(2,1)} %param.31) | copy-start | bytes 772
  0.7 5.7 %copy-start.60 = (bf16[1024]{0:T(1024)(128)(2,1)S(1)}, bf16[1024]{0:T(1024)(128)(2,1)}, u32[]{:S(2)}) copy-start(bf16[1024]{0:T(1024)(128)(2,1)} %param.29) | copy-start | bytes 6148
  0.7 5.7 %copy-start.65 = (bf16[128]{0:T(256)(128)(2,1)S(1)}, bf16[128]{0:T(256)(128)(2,1)}, u32[]{:S(2)}) copy-start(bf16[128]{0:T(256)(128)(2,1)} %param.27) | copy-start | bytes 772
  0.7 5.7 %copy-start.64 = (bf16[128]{0:T(256)(128)(2,1)S(1)}, bf16[128]{0:T(256)(128)(2,1)}, u32[]{:S(2)}) copy-start(bf16[128]{0:T(256)(128)(2,1)} %param.26) | copy-start | bytes 772
  0.7 5.7 %copy-start.63 = (bf16[128]{0:T(256)(128)(2,1)S(1)}, bf16[128]{0:T(256)(128)(2,1)}, u32[]{:S(2)}) copy-start(bf16[128]{0:T(256)(128)(2,1)} %param.25) | copy-start | bytes 772
  0.7 5.7 %copy-start.62 = (bf16[128]{0:T(256)(128)(2,1)S(1)}, bf16[128]{0:T(256)(128)(2,1)}, u32[]{:S(2)}) copy-start(bf16[128]{0:T(256)(128)(2,1)} %param.21) | copy-start | bytes 772
  0.7 5.7 %copy-start.61 = (bf16[128]{0:T(256)(128)(2,1)S(1)}, bf16[128]{0:T(256)(128)(2,1)}, u32[]{:S(2)}) copy-start(bf16[128]{0:T(256)(128)(2,1)} %param.20) | copy-start | bytes 772
  0.7 5.9 %copy-start.53 = (bf16[146,2,1024]{2,1,0:T(2,128)(2,1)S(1)}, bf16[146,2,1024]{2,1,0:T(2,128)(2,1)}, u32[]{:S(2)}) copy-start(bf16[146,2,1024]{2,1,0:T(2,128)(2,1)} %param.17) | copy-start | bytes 1794052
  172.2 8.3 %copy-start = (bf16[12,4,2,128,1024]{4,3,2,1,0:T(8,128)(2,1)}, bf16[12,4,2,128,1024]{4,3,2,1,0:T(8,128)(2,1)S(1)}, u32[]{:S(2)}) copy-start(bf16[12,4,2,128,1024]{4,3,2,1,0:T(8,128)(2,1)S(1)} %get-tuple-element.29) | copy-start | bytes 75497472
  207.3 4.9 %copy-start.1 = (bf16[640,1024]{1,0:T(8,128)(2,1)}, bf16[640,1024]{1,0:T(8,128)(2,1)S(1)}, u32[]{:S(2)}) copy-start(bf16[640,1024]{1,0:T(8,128)(2,1)S(1)} %add_convert_fusion.1.v) | copy-start | bytes 3932164
  207.3 3.0 copy-start.17
  207.5 4.7 copy-start.6
  212.2 11.9 %copy-start.19 = (bf16[1,4,2,128,1024]{4,3,2,1,0:T(8,128)(2,1)S(1)}, bf16[1,4,2,128,1024]{4,3,2,1,0:T(8,128)(2,1)}, u32[]{:S(2)}) copy-start(bf16[1,4,2,128,1024]{4,3,2,1,0:T(8,128)(2,1)} %get-tuple-element.104) | copy-start | bytes 6291460
  225.4 35.4 %copy-start.3 = (f32[320,1024]{0,1:T(8,128)}, f32[320,1024]{0,1:T(8,128)S(1)}, u32[]{:S(2)}) copy-start(f32[320,1024]{0,1:T(8,128)S(1)} %get-tuple-element.132) | copy-start | bytes 3932164
  225.7 1.9 copy-start.16
  228.4 5.6 %copy-start.29 = (f32[320,1024]{1,0:T(8,128)}, f32[320,1024]{1,0:T(8,128)S(1)}, u32[]{:S(2)}) copy-start(f32[320,1024]{1,0:T(8,128)S(1)} %convolution_add_fusion.3) | copy-start | bytes 3932164
  234.1 1.8 copy-start.15
  236.8 5.4 %copy-start.27 = (f32[320,1024]{1,0:T(8,128)}, f32[320,1024]{1,0:T(8,128)S(1)}, u32[]{:S(2)}) copy-start(f32[320,1024]{1,0:T(8,128)S(1)} %convolution_add_fusion.2) | copy-start | bytes 3932164
  244.8 5.4 %copy-start.25 = (f32[320,1024]{1,0:T(8,128)}, f32[320,1024]{1,0:T(8,128)S(1)}, u32[]{:S(2)}) copy-start(f32[320,1024]{1,0:T(8,128)S(1)} %convolution_add_fusion.1) | copy-start | bytes 3932164
  250.2 1.8 copy-start.8
  252.9 5.9 %copy-start.23 = (f32[320,1024]{1,0:T(8,128)}, f32[320,1024]{1,0:T(8,128)S(1)}, u32[]{:S(2)}) copy-start(f32[320,1024]{1,0:T(8,128)S(1)} %convolution_add_fusion) | copy-start | bytes 3932164
  258.8 2.0 copy-start.32
  258.8 2.1 copy-start.22
  293.0 5.5 %collective-permute-start = (bf16[320,2048]{1,0:T(8,128)(2,1)}, bf16[320,2048]{1,0:T(8,128)(2,1)}, u32[]{:S(2)}, u32[]{:S(2)}) collective-permute-start(bf16[320,2048]{1,0:T(8,128)(2,1)} %constant_dynamic-slice_fusion.2), channel_id=1, source_target_pairs={{0,4},{4,0},{8,12},{12,8},{16,20},{20,16},{24,28},{28,24},{1,5},{5... | collective-permute-start | bytes 3932168 | tf_op jit(solution)/shard_map/ppermute | solution.py:1056
  295.3 1.9 copy-start.18
  298.5 2.4 copy-start.42
  300.9 2.4 copy-start.13
  303.3 1.9 copy-start.10
  315.1 2.2 copy-start.46
  327.9 2.3 copy-start.21
  472.6 3.2 copy-start.56
  (36 other events, 55.8 us)

commit v2 on v1

--- a/solution.py
+++ b/solution.py
@@ -497,8 +497,10 @@
             self.far_in(way).wait_recv()
         self.pair(self.c).start()
 
+    def ready(self):
+        self.pair(1 - self.c).wait_recv()
+
     def finish(self):
-        self.pair(1 - self.c).wait_recv()
         t = self.t
         for k in range(T):
 
@@ -516,53 +518,271 @@
         self.pair(self.c).wait_send()
 
 
-def gather_kernel(
-    w, v, x, cot, valid, full_w, full_v, full_x, full_cot, full_valid, *sems
+LAGS = (1, 2, 3, 5, 7)
+ORDER = (0, 1, 2, 3, 4, 8, 5, 9, 6, 10, 7, 11)
+QUARTERS = 4
+TILE = 256
+
+
+def tiles(n, size, body):
+    def run(i, carry):
+        body(pl.ds(pl.multiple_of(i * size, size), size), i)
+        return carry
+
+    lax.fori_loop(0, n // size, run, 0)
+
+
+def to_lanes(a):
+    return a.astype(F32).T.astype(BF16)
+
+
+def matrix(w, j, cols=None):
+    a = w[j] if cols is None else w[j, :, :, :, cols]
+    return a.reshape(D, a.shape[-1])
+
+
+def matrix_rows(w, j, n):
+    return w[j, n].reshape(2 * ROWS, D)
+
+
+def forward_kernel(
+    w, v, x, cot, valid,
+    o_w, o_vec, o_x, o_cot, o_bias, o_q, o_k, o_v, o_att, o_nt, o_n2t, o_mgt, o_hid, o_pre,
+    o_n2g, o_resid, o_blk, o_ups,
+    gw, gv, xf, cf, mf, vec, bias, normed, q_s, k_s, v_s, att, resid, n2, nt, n2t, mgt, hid, pre,
+    n2g, mlp, slope, blk, ups,
+    ex_sem, mask_sem, pass_sem, out_sem, *chunk_sems,
 ):
-    ex_sem, mask_sem, pass_sem, chunk_sems = sems[0], sems[1], sems[2], sems[3:]
     spot = place()
     d, t, c, p, px, py, pd = spot
     greet(d, t, c, p, px, py)
     partner = (2 * p + 1 - c, t)
-    swap_x = Exchange(x, full_x, ex_sem.at[0], ex_sem.at[1], spot, True)
-    swap_c = Exchange(cot, full_cot, ex_sem.at[2], ex_sem.at[3], spot, False)
-    swap_x.start()
-    mask_out = remote(valid, full_valid.at[c], mask_sem.at[0], mask_sem.at[1], partner)
-    mask_in = remote(valid, full_valid.at[1 - c], mask_sem.at[0], mask_sem.at[1], partner)
-    mask_own = pltpu.make_async_copy(valid, full_valid.at[c], mask_sem.at[2])
-    mask_out.start()
-    mask_own.start()
+    swap_x = Exchange(x, xf, ex_sem.at[0], ex_sem.at[1], spot, True)
+    swap_c = Exchange(cot, cf, ex_sem.at[2], ex_sem.at[3], spot, False)
+    mask_out = remote(valid, mf.at[c], mask_sem.at[0], mask_sem.at[1], partner)
+    mask_in = remote(valid, mf.at[1 - c], mask_sem.at[0], mask_sem.at[1], partner)
+    mask_own = pltpu.make_async_copy(valid, mf.at[c], mask_sem.at[2])
 
     def passed(core, k):
-        view = full_x.at[2 * core + k]
+        view = xf.at[2 * core + k]
         return remote(view, view, pass_sem.at[0, k], pass_sem.at[1, k], partner)
 
-    chunks = [Gather(v, full_v, chunk_sems, 0, spot)]
-    for j in range(TILES):
-        chunks.append(Gather(w.at[j], full_w.at[j], chunk_sems, j + 1, spot))
+    chunks = [Gather(v, gv, chunk_sems, 0, spot)]
+    for i, j in enumerate(ORDER):
+        chunks.append(Gather(w.at[j], gw.at[j], chunk_sems, i + 1, spot))
     count = len(chunks)
-    for s in range(count + 6):
+
+    def comm(s):
         for lag, stage in (
-            (5, lambda g: g.ring_three()),
-            (4, lambda g: g.ring_two()),
-            (3, lambda g: (g.hop(3), g.ring_one())),
-            (2, lambda g: g.hop(2)),
-            (1, lambda g: g.hop(1)),
+            (LAGS[4], lambda g: g.ring_three()),
+            (LAGS[3], lambda g: g.ring_two()),
+            (LAGS[2], lambda g: (g.hop(3), g.ring_one())),
+            (LAGS[1], lambda g: g.hop(2)),
+            (LAGS[0], lambda g: g.hop(1)),
             (0, lambda g: g.own()),
         ):
             if 0 <= s - lag < count:
                 stage(chunks[s - lag])
-        if s == 0:
-            swap_c.start()
-        if s == 3:
+        if s == 1:
+            swap_x.start()
+            mask_out.start()
+            mask_own.start()
+        if s == 4:
             for k in range(2):
                 swap_x.wait_in(k)
                 passed(c, k).start()
-    for k in range(2):
-        swap_c.wait_in(k)
-        passed(1 - c, k).wait_recv()
-    mask_in.wait_recv()
-    mask_own.wait()
+        if s == 8:
+            swap_c.start()
+
+    nq = q_s.shape[0]
+    nk = k_s.shape[0]
+    block = xf.shape[1]
+    own_rows = pl.ds(pl.multiple_of(c * nq, nq), nq)
+    copies = []
+
+    def emit(src, dst):
+        copy = pltpu.make_async_copy(src, dst, out_sem.at[len(copies)])
+        copy.start()
+        copies.append(copy)
+
+    def vectors():
+        for q in range(NP):
+            for core in range(2):
+                part = gv[q, core].astype(F32)
+                first = (2 * q + core) * ROWS
+                vec[0:6, first : first + ROWS] = part[0:6, 0:ROWS]
+        part = gv[0, 0].astype(F32)
+        per = COLS // 128
+        for i in range(2 + QUARTERS):
+            for tau in range(T):
+                for r in range(per):
+                    row = 6 + i * per + r
+                    at = tau * COLS + r * 128
+                    vec[6 + i : 7 + i, at : at + 128] = part[row : row + 1, tau * 128 : tau * 128 + 128]
+        emit(vec, o_vec)
+        mask_in.wait_recv()
+        mask_own.wait()
+        rows = mf[t // 2].T
+        col = jnp.where(lax.rem(t, 2) == 0, rows[:, 0:1], rows[:, 1:2])
+        bias[...] = jnp.where(col > 0, 0.0, NEG).astype(F32)
+        emit(bias, o_bias)
+
+    def norm_one():
+        for k in range(2):
+            passed(1 - c, k).wait_recv()
+        emit(xf.at[pl.ds(2 * c, 2)], o_x)
+        size = 32
+        per = block // size
+
+        def run(i, carry):
+            at = pl.ds(pl.multiple_of(lax.rem(i, per) * size, size), size)
+            unit, unused = norm_parts(xf[i // per, at].astype(F32))
+            normed[pl.ds(pl.multiple_of(i * size, size), size)] = (
+                unit * vec[0:1] + vec[1:2]
+            ).astype(BF16)
+            return carry
+
+        lax.fori_loop(0, nk // size, run, 0)
+
+        def flip(cols, i):
+            nt[cols] = to_lanes(normed[own_rows, cols])
+
+        tiles(D, TILE, flip)
+        emit(nt, o_nt)
+
+    def project(j, dst, rows, shift):
+        a = normed[rows]
+
+        def run(cols, i):
+            out = jnp.dot(a, matrix(gw, j, cols), preferred_element_type=F32)
+            if shift is not None:
+                out = out + vec[shift : shift + 1, cols]
+            dst[:, cols] = out.astype(BF16)
+
+        tiles(D, TILE, run)
+
+    def heads(first, last):
+        def run(i, carry):
+            cols = pl.ds(pl.multiple_of(i * 2 * HD, 2 * HD), 2 * HD)
+            q_t = (q_s[:, cols].astype(F32).T * HD ** (-0.5)).astype(BF16)
+            v_t = to_lanes(v_s[:, cols])
+            k = k_s[:, cols]
+            parts = []
+            for h in range(2):
+                probs = head_probs(k, head_rows(q_t, h), bias[...]).astype(BF16)
+                parts.append(
+                    jnp.dot(v_t[h * HD : (h + 1) * HD], probs, preferred_element_type=F32)
+                )
+            att[:, cols] = jnp.concatenate(parts, axis=0).T.astype(BF16)
+            return carry
+
+        lax.fori_loop(first, last, run, 0)
+
+    def middle():
+        emit(att, o_att)
+        a = att[...]
+        x_own = xf.at[pl.ds(2 * c, 2)]
+
+        def run(cols, i):
+            out = dot_nt(a, matrix_rows(gw, 3, i))
+            resid[:, cols] = (
+                x_own[:, :, cols].astype(F32).reshape(nq, TILE) + out + vec[2:3, cols]
+            )
+
+        tiles(D, TILE, run)
+        emit(resid, o_resid)
+
+        def norm(rows, i):
+            unit, unused = norm_parts(resid[rows])
+            n2[rows] = (unit * vec[3:4] + vec[4:5]).astype(BF16)
+
+        tiles(nq, 64, norm)
+
+        def flip(cols, i):
+            n2t[cols] = to_lanes(n2[:, cols])
+
+        tiles(D, TILE, flip)
+        emit(n2t, o_n2t)
+
+    def grads_in():
+        for k in range(2):
+            swap_c.wait_in(k)
+        emit(cf, o_cot)
+
+        def flip(cols, i):
+            mgt[cols] = to_lanes(cf[:, :, cols].reshape(nq, TILE))
+
+        tiles(D, TILE, flip)
+        emit(mgt, o_mgt)
+
+    def quarter_up(j):
+        a = n2[...]
+
+        def run(cols, i):
+            z = jnp.dot(a, matrix(gw, 4 + j, cols), preferred_element_type=F32)
+            z = z + vec[8 + j : 9 + j, cols]
+            share = 0.5 + 0.5 * lax.erf(z * 0.5**0.5)
+            hid[j, :, cols] = (z * share).astype(BF16)
+            slope[:, cols] = share + z * (jnp.exp(-0.5 * z * z) * (0.5 / jnp.pi) ** 0.5)
+
+        tiles(D, TILE, run)
+        emit(hid.at[j], o_hid.at[j])
+
+    def quarter_down(j):
+        g = cf[...].reshape(nq, D)
+
+        def back(cols, i):
+            h = jnp.dot(g, matrix(gw, 8 + j, cols), preferred_element_type=F32)
+            grad = (slope[:, cols] * h).astype(BF16)
+            pre[j, :, cols] = grad
+            ups[j : j + 1, cols] = jnp.sum(grad.astype(F32), axis=0, keepdims=True)
+
+        tiles(D, TILE, back)
+        emit(pre.at[j], o_pre.at[j])
+
+        def outs(cols, i):
+            m = dot_nt(hid[j], matrix_rows(gw, 8 + j, i))
+            n = dot_nt(pre[j], matrix_rows(gw, 4 + j, i))
+            if j == 0:
+                mlp[:, cols] = m
+                n2g[:, cols] = n
+            elif j < QUARTERS - 1:
+                mlp[:, cols] += m
+                n2g[:, cols] += n
+            else:
+                n2g[:, cols] += n
+                blk[:, cols] = (resid[:, cols] + mlp[:, cols] + m + vec[5:6, cols]).astype(BF16)
+
+        tiles(D, TILE, outs)
+
+    whole = pl.ds(0, nk)
+    after = {
+        8: (vectors, norm_one),
+        9: (lambda: project(0, q_s, own_rows, 6), lambda: emit(q_s, o_q)),
+        10: (lambda: project(1, k_s, whole, None), lambda: emit(k_s, o_k)),
+        11: (lambda: project(2, v_s, whole, 7), lambda: emit(v_s, o_v), lambda: heads(0, 2)),
+        12: (lambda: heads(2, 6),),
+        13: (lambda: heads(6, 8), middle),
+        14: (lambda: quarter_up(0), grads_in, lambda: quarter_down(0)),
+        15: (lambda: quarter_up(1),),
+        16: (lambda: quarter_down(1),),
+        17: (lambda: quarter_up(2),),
+        18: (lambda: quarter_down(2),),
+        19: (lambda: quarter_up(3),),
+        20: (lambda: quarter_down(3),),
+    }
+    for s in range(count + LAGS[4] + 1):
+        comm(s)
+        if 0 <= s - LAGS[4] - 1 < count:
+            i = s - LAGS[4] - 1
+            chunks[i].ready()
+            if 1 <= i <= 4:
+                emit(gw.at[ORDER[i - 1]], o_w.at[ORDER[i - 1]])
+        for unit in after.get(s, ()):
+            unit()
+    emit(n2g, o_n2g)
+    emit(blk, o_blk)
+    emit(ups, o_ups)
     for chunk in chunks:
         chunk.finish()
     for k in range(2):
@@ -570,28 +790,79 @@
         swap_x.wait_out(k)
         swap_c.wait_out(k)
     mask_out.wait_send()
-
-
-def gather_all(w, v, x, cot, valid):
+    for copy in copies:
+        copy.wait()
+
+
+def forward_all(w, v, x, cot, valid):
     any_space = pl.BlockSpec(memory_space=pl.ANY)
     dma = pltpu.SemaphoreType.DMA
     n = TILES + 1
-    lead = NP, 2
+    block = x.shape[1]
+    nk = T * block
+    nq = nk // 2
+    gathered = (NP, 2, ROWS, D)
+
+    def half(rows, cols=D):
+        return (rows, cols), BF16
+
+    outs = (
+        ((4,) + gathered, BF16),
+        ((16, D), F32),
+        ((2, block, D), BF16),
+        ((2, block, D), BF16),
+        ((nk, 1), F32),
+        half(nq),
+        half(nk),
+        half(nk),
+        half(nq),
+        half(D, nq),
+        half(D, nq),
+        half(D, nq),
+        ((QUARTERS, nq, D), BF16),
+        ((QUARTERS, nq, D), BF16),
+        ((nq, D), F32),
+        ((nq, D), F32),
+        half(nq),
+        ((8, D), F32),
+    )
+    scratch = (
+        ((TILES,) + gathered, BF16),
+        ((NP, 2, VROWS, 128 * T), BF16),
+        ((T, block, D), BF16),
+        ((2, block, D), BF16),
+        ((2,) + valid.shape, F32),
+        ((16, D), F32),
+        ((nk, 1), F32),
+        half(nk),
+        half(nq),
+        half(nk),
+        half(nk),
+        half(nq),
+        ((nq, D), F32),
+        half(nq),
+        half(D, nq),
+        half(D, nq),
+        half(D, nq),
+        ((QUARTERS, nq, D), BF16),
+        ((QUARTERS, nq, D), BF16),
+        ((nq, D), F32),
+        ((nq, D), F32),
+        ((nq, D), F32),
+        half(nq),
+        ((8, D), F32),
+    )
     return pl.pallas_call(
-        gather_kernel,
-        out_shape=(
-            jax.ShapeDtypeStruct((TILES,) + lead + (ROWS, D), BF16),
-            jax.ShapeDtypeStruct(lead + (VROWS, 128 * T), BF16),
-            jax.ShapeDtypeStruct((T,) + x.shape[1:], BF16),
-            jax.ShapeDtypeStruct(cot.shape, BF16),
-            jax.ShapeDtypeStruct((2,) + valid.shape, F32),
-        ),
+        forward_kernel,
+        out_shape=[jax.ShapeDtypeStruct(*o) for o in outs],
         in_specs=[any_space] * 5,
-        out_specs=[any_space] * 5,
-        scratch_shapes=[
+        out_specs=[any_space] * len(outs),
+        scratch_shapes=[pltpu.VMEM(*o) for o in scratch]
+        + [
             dma((4, 2)),
             dma((3,)),
             dma((2, 2)),
+            dma((32,)),
             dma((n, T)),
             dma((n, 2, T)),
             dma((n,)),
@@ -600,8 +871,10 @@
             dma((n,)),
             dma((n,)),
         ],
-        name="gather_all",
-        compiler_params=pltpu.CompilerParams(collective_id=0, has_side_effects=True, vmem_limit_bytes=8 << 20),
+        name="forward_all",
+        compiler_params=pltpu.CompilerParams(
+            collective_id=0, has_side_effects=True, vmem_limit_bytes=60 << 20
+        ),
     )(w, v, x, cot, valid)
 
 
@@ -849,18 +1122,6 @@
     return jnp.where(lane == h, q, jnp.zeros_like(q))
 
 
-def attend_kernel(q, k, v, bias, out):
-    q_t = (q[...].astype(F32).T * HD ** (-0.5)).astype(BF16)
-    v_t = v[...].astype(F32).T.astype(BF16)
-    parts = []
-    for h in range(2):
-        probs = head_probs(k[...], head_rows(q_t, h), bias[...]).astype(BF16)
-        parts.append(
-            jnp.dot(v_t[h * HD : (h + 1) * HD], probs, preferred_element_type=F32)
-        )
-    out[...] = jnp.concatenate(parts, axis=0).T.astype(BF16)
-
-
 def attend_back_kernel(q, k, v, g, bias, dq, dk, dv):
     q_s = (q[...].astype(F32) * HD ** (-0.5)).astype(BF16)
     q_t = q_s.astype(F32).T.astype(BF16)
@@ -883,19 +1144,6 @@
 
 def columns(rows):
     return pl.BlockSpec((rows, 2 * HD), lambda i: (0, i))
-
-
-def attend(q, k, v, bias):
-    nq, nk = q.shape[0], k.shape[0]
-    return pl.pallas_call(
-        attend_kernel,
-        grid=(H // 2,),
-        out_shape=jax.ShapeDtypeStruct((nq, D), BF16),
-        in_specs=[columns(nq), columns(nk), columns(nk), pl.BlockSpec((nk, 1), lambda i: (0, 0))],
-        out_specs=columns(nq),
-        name="attend",
-        compiler_params=pltpu.CompilerParams(vmem_limit_bytes=48 << 20),
-    )(q, k, v, bias)
 
 
 def attend_back(q, k, v, g, bias):
@@ -990,29 +1238,14 @@
         axis=0,
     )
     v = jnp.pad(v, ((0, VROWS - v.shape[0]), (0, 0)))
-    full_w, full_v, full_x, own_cot, full_valid = gather_all(w, v, x_blocks, c_blocks, valid)
-    g = full_w.reshape(TILES, D, D)
-    vectors = full_v[:, :, :6, :128].astype(F32)
-    gain_one, shift_one, proj_b, gain_two, shift_two, down_b = [
-        vectors[:, :, i].reshape(1, D) for i in range(6)
-    ]
-    split = full_v[0, 0].reshape(VROWS, T, 128).astype(F32)
-    per_tau = COLS // 128
-
-    def spread_out(first, count):
-        part = split[first : first + count * per_tau].reshape(count, per_tau, T, 128)
-        return jnp.transpose(part, (0, 2, 1, 3)).reshape(count, 1, D)
-
-    attn_b = spread_out(6, 2)
-    up_b = spread_out(6 + 2 * per_tau, per_j)
-
-    nk = T * block
-    nq = nk // 2
-    x_all = full_x.reshape(nk, D).astype(F32)
-    image_valid = lax.dynamic_slice(
-        full_valid, (t // 2, lax.rem(t, 2), 0), (1, 1, nk)
-    ).reshape(nk, 1)
-    bias = jnp.where(image_valid > 0, 0.0, NEG).astype(F32)
+    (
+        full_w, vec, x_own, own_cot, bias, queries, keys, values, attended, normed_t, normed2_t,
+        mlp_grad_t, hidden, pre_grad, normed2_grad, resid, block_own, up_sums,
+    ) = forward_all(w, v, x_blocks, c_blocks, valid)
+    g = full_w.reshape(4, D, D)
+    nq = resid.shape[0]
+    gain_one, gain_two = vec[0:1], vec[3:4]
+    unit_one, inverse_one = norm_parts(x_own.reshape(nq, D).astype(F32))
 
     def mine(a):
         return lax.dynamic_slice_in_dim(a, c * nq, nq, 0)
@@ -1020,33 +1253,8 @@
     def other(a):
         return lax.dynamic_slice_in_dim(a, (1 - c) * nq, nq, 0)
 
-    unit_all, inverse_all = norm_parts(x_all)
-    normed_all = (unit_all * gain_one + shift_one).astype(BF16)
-    normed = mine(normed_all)
-    x_own = mine(x_all)
-    queries = (dot_nn(normed, g[0]) + attn_b[0]).astype(BF16)
-    keys = dot_nn(normed_all, g[1]).astype(BF16)
-    values = (dot_nn(normed_all, g[2]) + attn_b[1]).astype(BF16)
-    attended = attend(queries, keys, values, bias)
-    resid = x_own + dot_nt(attended, g[3]) + proj_b
     unit_two, inverse_two = norm_parts(resid)
-    normed2 = (unit_two * gain_two + shift_two).astype(BF16)
-    mlp_grad = own_cot.reshape(nq, D)
-    outer = mlp_grad.astype(F32)
-    hidden, pre_grad, up_sums = [], [], []
-    mlp_out = jnp.zeros((nq, D), F32)
-    normed2_grad = jnp.zeros((nq, D), F32)
-    for j in range(per_j):
-        hidden_pre = dot_nn(normed2, g[4 + j]) + up_b[j]
-        act, back = jax.vjp(gelu_exact, hidden_pre)
-        act = act.astype(BF16)
-        hidden.append(act)
-        mlp_out = mlp_out + dot_nt(act, g[8 + j])
-        grad = back(dot_nn(mlp_grad, g[8 + j]))[0].astype(BF16)
-        pre_grad.append(grad)
-        up_sums.append(jnp.sum(grad.astype(F32), axis=0))
-        normed2_grad = normed2_grad + dot_nt(grad, g[4 + j])
-    block_own = (resid + mlp_out + down_b).astype(BF16)
+    outer = own_cot.reshape(nq, D).astype(F32)
     resid_grad = outer + norm_back(normed2_grad, unit_two, inverse_two, gain_two)
     branch = resid_grad.astype(BF16)
     att_grad = dot_nn(branch, g[3]).astype(BF16)
@@ -1057,7 +1265,6 @@
     dkv = (mine(dkv).astype(F32) + came.astype(F32)).astype(BF16)
     dk, dv = dkv[:, :D], dkv[:, D:]
     normed_grad = dot_nt(dq, g[0]) + dot_nt(dk, g[1]) + dot_nt(dv, g[2])
-    unit_one, inverse_one = mine(unit_all), mine(inverse_all)
     input_own = resid_grad + norm_back(normed_grad, unit_one, inverse_one, gain_one)
     sums = jnp.stack(
         [
@@ -1070,10 +1277,10 @@
             jnp.sum(dq.astype(F32), axis=0),
             jnp.sum(dv.astype(F32), axis=0),
         ]
-        + up_sums
+        + [up_sums[j] for j in range(QUARTERS)]
     )
-    at = jnp.stack([jnp.transpose(a) for a in (normed, branch, normed2, mlp_grad)])
-    b = jnp.stack([dq, dk, dv, attended] + pre_grad + hidden)
+    at = jnp.stack([normed_t, jnp.transpose(branch), normed2_t, mlp_grad_t])
+    b = jnp.concatenate([jnp.stack([dq, dk, dv, attended]), pre_grad, hidden], axis=0)
     grads, totals, own_block, own_input = scatter_all(
         at,
         b,

time: 490 us -> 377 us (0.77)
  matrix products: 45.4 us -> 5.37 us
  Pallas kernels: 334 us -> 301 us
  local copies, waits for them, and re-layouts: 83.6 us -> 52.1 us
    pallas_call x2 -> x1, Pallas kernels: 176 us -> 143 us  [forward_all(): pl.pallas_call(forward_kernel, out_shape=[jax.ShapeDtypeStruct(*o) for o...]
    dot_general x12 -> x1, matrix products: 28.5 us -> 0.89 us  [dot_nn(): lax.dot_general(a, b, (((1,), (0,)), ((), ())), preferred_element_type=F32)]
    unnamed x152 -> x95, local copies, waits for them, and re-layouts: 45.4 us -> 19.2 us
    dot_general x12 -> x3, matrix products: 16.9 us -> 4.49 us  [dot_nt(): lax.dot_general(a, b, (((1,), (1,)), ((), ())), preferred_element_type=F32)]
    slice x6 -> x3, local copies, waits for them, and re-layouts: 17.5 us -> 7.15 us  [the longest x1 5.69 us: per_device_chips(): normed_grad = dot_nt(dq, g[0]) + dot_nt(dk, g[1]) + dot_nt(dv, g[2])]
where the time goes in v2:
time: 377 us; the launch traced here: 376 us
  Pallas kernels  301 us (80%)
  local copies, waits for them, and re-layouts  52.1 us (14%)
  other arithmetic  15 us (4%)
  matrix products  5.37 us (1%)
    pallas_call x1, Pallas kernels, forward_all(): pl.pallas_call(forward_kernel, out_shape=[jax.ShapeDtypeStruct(*o) for o...  143 us
    pallas_call x1, Pallas kernels, scatter_all(): pl.pallas_call(scatter_kernel, out_shape=(jax.ShapeDtypeStruct((n, ROWS,...  136 us
    pallas_call x1, Pallas kernels, attend_back(): pl.pallas_call(attend_back_kernel, grid=(H // 2,), out_shape=(jax.ShapeDt...  22.2 us
    unnamed x95, local copies, waits for them, and re-layouts  19.2 us
  transfers between devices with their start and end apart: 1, of which 0 were waited for; matrix products, arithmetic and copies ran while one was open for 1% of the time, Pallas kernels for 0%

profile of v2, /device:TPU:0, one launch (start us, length us, event | category | flops | bytes accessed | tf_op | source)
XLA Modules:
  0.0 376.2 jit_solution(323143785613817211)
XLA Ops:
  4.6 1.1 copy.46
  5.9 1.1 copy.48
  8.9 1.0 pad.21.cot
  10.0 1.0 pad.20.x
  12.0 143.0 %forward_all.1 = (bf16[4,4,2,128,1024]{4,3,2,1,0:T(8,128)(2,1)}, f32[16,1024]{1,0:T(8,128)}, bf16[2,160,1024]{2,1,0:T(8,128)(2,1)}, bf16[2,160,1024]{2,1,0:T(8,1...) custom-call(bf16[12,128,256]{2,1,0:T(8,128)(2,1)} %pad_maximum_fusio, ...), custom_call_target="tpu_custom_call" | custom-call | tf_op jit(solution)/shard_map/forward_all/pallas_call | solution.py:855
  155.0 1.6 reduce_sum.144
  158.3 1.8 copy.52
  160.1 2.5 copy.53
  162.6 5.7 %fusion.6 = (bf16[1,4,2,128,1024]{4,3,2,1,0:T(8,128)(2,1)}, bf16[1,4,2,128,1024]{4,3,2,1,0:T(8,128)(2,1)}, bf16[1,4,2,128,1024]{4,3,2,1,0:T(8,128)(2,1)}, bf16[1,4,2,128,1024]{4,3,2,1,0:T(8,128)(2,1)S(1)}) fusion(bf16[4,4,2,128,1024]{4,3,2,1,0:T(8,128)(2,1)} %get-tuple-element.49), kind=kLoop, calls=%fused_computation.63 | loop fusion | bytes 16777216 | tf_op jit(solution)/shard_map/slice | solution.py:1267
  168.3 1.2 multiply_reduce_fusion.1
  169.7 1.3 convert_reduce_fusion
  173.1 22.2 %attend_back.1 = (bf16[320,1024]{1,0:T(8,128)(2,1)S(1)}, bf16[640,1024]{1,0:T(8,128)(2,1)S(1)}, bf16[640,1024]{1,0:T(8,128)(2,1)S(1)}) custom-call(bf16[320,1024]{1,0:T(8,128)(2,1)S(1)} %copy-done.1, bf16[640,1024]{1,0:T(8,128)(2,1)S(1)} %copy-done, bf16[640,1024]{1,0:T(8,128)(2,1)} %get-tuple-element.48.v, bf16[320,1024]{1,0:T(8,128)(2,1)S(1)} %convolution_convert_fusion.g, ...), custom_call_target="tpu_custom_call" | custom-call | tf_op jit(solution)/shard_map/attend_back/pallas_call | solution.py:1151
  195.3 1.2 constant_dynamic-update-slice_fusion.1
  196.4 1.2 constant_dynamic-update-slice_fusion
  197.7 2.7 constant_dynamic-slice_fusion.1
  205.4 1.3 fusion.8
  207.1 1.9 add_convert_fusion
  209.2 1.3 fusion.2
  210.8 2.0 multiply_reduce_fusion
  212.8 1.7 add_convert_fusion.1
  214.5 2.2 copy.59
  220.5 1.8 constant_dynamic-update-slice_fusion.3
  223.2 1.7 constant_dynamic-update-slice_fusion.2.b
  225.9 2.0 pad_maximum_fusion.at
  228.0 135.7 %scatter_all.1 = (f32[12,128,256]{2,1,0:T(8,128)}, f32[96,128]{1,0:T(8,128)}, bf16[2,160,1024]{2,1,0:T(8,128)(2,1)}, bf16[2,160,1024]{2,1,0:T(8,128)(2,1)}) custom-call(bf16[4,1024,320]{2,1,0:T(8,128)(2,1)} %pad_maximum_fusion.at, bf16[12,320,1024]{2,1,0:T(8,128)(2,1)} %constant_dynamic-update-slice_fusion.2.b, f32[96,128]{1,0:T(8,128)} %reshape.154.vec, ...), custom_call_target="tpu_custom_call" | custom-call | tf_op jit(solution)/shard_map/scatter_all/pallas_call | solution.py:1076
  363.7 1.0 slice_bitcast_fusion.2
  364.7 1.8 slice.90
  366.5 1.3 slice_bitcast_fusion
  368.0 1.4 copy.62
  372.0 1.0 copy.61
  373.2 1.0 copy.65
  374.3 1.9 copy.63
  (134 shorter events, 24.7 us)
Async XLA Ops:
  0.6 7.2 %copy-start.39 = (bf16[128]{0:T(256)(128)(2,1)S(1)}, bf16[128]{0:T(256)(128)(2,1)}, u32[]{:S(2)}) copy-start(bf16[128]{0:T(256)(128)(2,1)} %param.31) | copy-start | bytes 772
  0.7 7.2 %copy-start.33 = (bf16[1024]{0:T(1024)(128)(2,1)S(1)}, bf16[1024]{0:T(1024)(128)(2,1)}, u32[]{:S(2)}) copy-start(bf16[1024]{0:T(1024)(128)(2,1)} %param.29) | copy-start | bytes 6148
  0.7 7.1 %copy-start.38 = (bf16[128]{0:T(256)(128)(2,1)S(1)}, bf16[128]{0:T(256)(128)(2,1)}, u32[]{:S(2)}) copy-start(bf16[128]{0:T(256)(128)(2,1)} %param.27) | copy-start | bytes 772
  0.7 7.1 %copy-start.37 = (bf16[128]{0:T(256)(128)(2,1)S(1)}, bf16[128]{0:T(256)(128)(2,1)}, u32[]{:S(2)}) copy-start(bf16[128]{0:T(256)(128)(2,1)} %param.26) | copy-start | bytes 772
  0.7 7.1 %copy-start.36 = (bf16[128]{0:T(256)(128)(2,1)S(1)}, bf16[128]{0:T(256)(128)(2,1)}, u32[]{:S(2)}) copy-start(bf16[128]{0:T(256)(128)(2,1)} %param.25) | copy-start | bytes 772
  0.7 7.1 %copy-start.35 = (bf16[128]{0:T(256)(128)(2,1)S(1)}, bf16[128]{0:T(256)(128)(2,1)}, u32[]{:S(2)}) copy-start(bf16[128]{0:T(256)(128)(2,1)} %param.21) | copy-start | bytes 772
  0.7 7.1 %copy-start.34 = (bf16[128]{0:T(256)(128)(2,1)S(1)}, bf16[128]{0:T(256)(128)(2,1)}, u32[]{:S(2)}) copy-start(bf16[128]{0:T(256)(128)(2,1)} %param.20) | copy-start | bytes 772
  0.7 8.0 %copy-start.21 = (bf16[146,2,1024]{2,1,0:T(2,128)(2,1)S(1)}, bf16[146,2,1024]{2,1,0:T(2,128)(2,1)}, u32[]{:S(2)}) copy-start(bf16[146,2,1024]{2,1,0:T(2,128)(2,1)} %param.17) | copy-start | bytes 1794052
  5.9 4.0 %copy-start.22 = (bf16[146,2,1024]{2,1,0:T(2,128)(2,1)S(1)}, bf16[146,2,1024]{2,1,0:T(2,128)(2,1)}, u32[]{:S(2)}) copy-start(bf16[146,2,1024]{2,1,0:T(2,128)(2,1)} %param.16) | copy-start | bytes 1794052
  171.0 1.9 copy-start
  171.0 2.0 copy-start.1
  171.0 2.1 copy-start.2
  197.7 3.6 copy-start.8
  197.7 3.8 %copy-start.9 = (f32[320,1024]{1,0:T(8,128)S(1)}, f32[320,1024]{1,0:T(8,128)}, u32[]{:S(2)}) copy-start(f32[320,1024]{1,0:T(8,128)} %get-tuple-element.42) | copy-start | bytes 3932164
  200.3 2.4 copy-start.32
  200.3 6.3 %collective-permute-start = (bf16[320,2048]{1,0:T(8,128)(2,1)}, bf16[320,2048]{1,0:T(8,128)(2,1)}, u32[]{:S(2)}, u32[]{:S(2)}) collective-permute-start(bf16[320,2048]{1,0:T(8,128)(2,1)} %constant_dynamic-slice_fusion.1), channel_id=1, source_target_pairs={{0,4},{4,0},{8,12},{12,8},{16,20},{20,16},{24,28},{28,24},{1,5},{5... | collective-permute-start | bytes 3932168 | tf_op jit(solution)/shard_map/ppermute | solution.py:1264
  203.6 1.8 copy-start.16
  206.6 2.5 copy-start.15
  210.8 2.0 copy-start.4
  212.8 4.0 %copy-start.26 = (f32[4,1024]{1,0:T(4,128)S(1)}, f32[4,1024]{1,0:T(4,128)}, u32[]{:S(2)}) copy-start(f32[4,1024]{1,0:T(4,128)} %slice.84) | copy-start | bytes 49156
  212.8 4.0 %copy-start.28 = (f32[1024]{0:T(1024)S(1)}, f32[1024]{0:T(1024)}, u32[]{:S(2)}) copy-start(f32[1024]{0:T(1024)} %get-tuple-element.94) | copy-start | bytes 12292
  212.8 4.0 %copy-start.29 = (f32[1024]{0:T(1024)S(1)}, f32[1024]{0:T(1024)}, u32[]{:S(2)}) copy-start(f32[1024]{0:T(1024)} %get-tuple-element.99) | copy-start | bytes 12292
  212.8 4.0 %copy-start.30 = (f32[1024]{0:T(1024)S(1)}, f32[1024]{0:T(1024)}, u32[]{:S(2)}) copy-start(f32[1024]{0:T(1024)} %reduce_sum.154) | copy-start | bytes 12292
  212.8 4.0 %copy-start.31 = (f32[1024]{0:T(1024)S(1)}, f32[1024]{0:T(1024)}, u32[]{:S(2)}) copy-start(f32[1024]{0:T(1024)} %convert_reduce_fusion.4) | copy-start | bytes 12292
  216.8 2.6 copy-start.20
  218.4 2.0 copy-start.13
  220.5 2.7 copy-start.12
  223.1 1.9 copy-start.17
  223.1 2.5 copy-start.18
  223.1 2.8 copy-start.19
  363.7 4.1 %copy-start.24 = (bf16[2,160,1024]{2,1,0:T(8,128)(2,1)S(1)}, bf16[2,160,1024]{2,1,0:T(8,128)(2,1)}, u32[]{:S(2)}) copy-start(bf16[2,160,1024]{2,1,0:T(8,128)(2,1)} %get-tuple-element.60) | copy-start | bytes 1966084
  372.0 2.2 copy-start.23
  (9 other events, 13.5 us)
